TPU v7x, 32 devices: a whole 2x2x4 slice. The times are simulated.
32 devices in a mesh: parts: 2 (over y), head: 16 (over z, x, core).
Axes of the slice: x: 2, y: 2, z: 4, core: 2. Of those that a mesh axis runs over, the one named last changes fastest.
Arguments:
- tokens: bfloat16 [512, 8192], P('parts', 'head'), parts along dimension 0, may hold values from -120 to 120
- pre_gain: bfloat16 [8192], P('head'), may hold values from 0.5 to 1.5
- w_in: bfloat16 [32, 256, 8192], P('head'), may hold values from -0.0625 to 0.0625
- w_dt: bfloat16 [32, 8192], P('head'), may hold values from -0.0625 to 0.0625
- dt_bias: float32 [32], P('head'), may hold values from -5 to -2
- a_log: float32 [32], P('head'), may hold values from -2.3 to 1.4
- conv_weight: bfloat16 [4, 32, 192], P(None, 'head'), may hold values from -3 to 3
- conv_bias: bfloat16 [32, 192], P('head'), may hold values from -2 to 2
- conv_tail: bfloat16 [6, 32, 192], P('parts', 'head'), parts along dimension 0, may hold values from -6 to 6
- init_state: float32 [64, 64, 256], P(('parts', 'head')), parts along dimension 0, may hold values from -0.6 to 0.6
- d_skip: float32 [32], P('head'), may hold values from 0.5 to 2
- norm_gain: bfloat16 [32, 64], P('head'), may hold values from 0.099609375 to 1.8984375
- w_out: bfloat16 [32, 64, 8192], P('head'), may hold values from -0.125 to 0.125
Outputs:
- mixer_out: bfloat16 [512, 8192], P('parts', 'head'), parts along dimension 0
- final_state: float32 [64, 64, 256], P(('parts', 'head')), parts along dimension 0
There are 2 independent parts, one for each index of `parts`. A program takes and returns all parts, laid end to end along the dimension named above; an argument that names none is the same for every part. Nothing has to cross between parts.
All inputs are finite; a program needn't handle non-finite values.
Results may differ from a plain program's by a relative error of at most 0.0073.
Values may be sent and summed in bfloat16 or wider, within the bound.
A program may use at most 64 MiB of HBM per device.

v0:
```python
import jax
import jax.numpy as jnp
from jax import lax
from jax.sharding import PartitionSpec as P

P_SIZE = 64
G = 8


epsilon = 1e-05


def from_partner(block, axis, apart):
    count = lax.axis_size(axis)
    route = []
    for low in range(count):
        high = low | 1 << apart
        if high != low and high < count:
            route += [(low, high), (high, low)]
    return lax.ppermute(block, axis, route)


def stretch_scan(x_values, dt_vals, decay_rate, b_matrix, c_matrix, start_state):
    seq_len = x_values.shape[0]
    heads_here = x_values.shape[1]
    block_len = 128
    block_count = seq_len // block_len
    precise = lax.Precision.HIGHEST
    log_steps = (dt_vals * decay_rate[None, :]).reshape(block_count, block_len, heads_here)
    cumlog = jnp.cumsum(log_steps, axis=1)
    x_blocks = x_values.reshape(block_count, block_len, heads_here, -1)
    dt_blocks = dt_vals.reshape(block_count, block_len, heads_here)
    b_blocks = b_matrix.reshape(block_count, block_len, -1)
    c_blocks = c_matrix.reshape(block_count, block_len, -1)
    positions = jnp.arange(block_len)
    causal = (positions[:, None] >= positions[None, :])[None, :, :, None]
    log_gaps = cumlog[:, :, None, :] - cumlog[:, None, :, :]
    decays = jnp.where(causal, jnp.exp(jnp.where(causal, log_gaps, 0.0)), 0.0)
    scores = jnp.einsum("cin,cjn->cij", c_blocks, b_blocks, precision=precise)
    mixing = scores[:, :, :, None] * decays * dt_blocks[:, None, :, :]
    inner_part = jnp.einsum("cijh,cjhp->cihp", mixing, x_blocks, precision=precise)
    tail_decay = jnp.exp(cumlog[:, -1:, :] - cumlog) * dt_blocks
    local_states = jnp.einsum(
        "cjh,cjhp,cjn->chpn", tail_decay, x_blocks, b_blocks, precision=precise
    )
    totals = jnp.exp(cumlog[:, -1, :])

    def advance(carried, element):
        total_now, added = element
        return (total_now[:, None, None] * carried + added, carried)

    final_state, entering = lax.scan(advance, start_state, (totals, local_states))
    outer_part = jnp.einsum("cin,chpn->cihp", c_blocks, entering, precision=precise)
    outer_part = outer_part * jnp.exp(cumlog)[:, :, :, None]
    return ((inner_part + outer_part).reshape(seq_len, heads_here, -1), final_state)


def per_device(
    tokens,
    pre_gain,
    w_in,
    w_dt,
    dt_bias,
    a_log,
    conv_weight,
    conv_bias,
    conv_tail,
    init_state,
    d_skip,
    norm_gain,
    w_out,
):
    seq_len = tokens.shape[0]
    heads_here = w_in.shape[0]
    width_full = w_in.shape[2]
    w_flat = w_in.reshape(-1, width_full)
    contract_last = (((1,), (1,)), ((), ()))
    rows_full, gain_full = (
        lax.all_gather(tokens, "head", axis=1, tiled=True),
        lax.all_gather(pre_gain, "head", axis=0, tiled=True),
    )
    wide_tokens = rows_full.astype(jnp.float32)
    row_scale = lax.rsqrt(jnp.mean(wide_tokens * wide_tokens, axis=1, keepdims=True) + epsilon)
    normed_in = (wide_tokens * row_scale * gain_full.astype(jnp.float32)).astype(jnp.bfloat16)
    proj_sum = lax.dot_general(normed_in, w_flat, contract_last, preferred_element_type=jnp.float32)
    dt_raw = lax.dot_general(normed_in, w_dt, contract_last, preferred_element_type=jnp.float32)
    projected = proj_sum.astype(jnp.bfloat16).reshape(seq_len, heads_here, -1)
    conv_in = jnp.concatenate([conv_tail, projected[:, :, P_SIZE:]], axis=0).astype(jnp.float32)
    convolved = jnp.zeros((seq_len,) + conv_bias.shape, jnp.float32) + conv_bias.astype(jnp.float32)
    for tap_index in range(conv_weight.shape[0]):
        convolved = (
            convolved
            + conv_weight[tap_index].astype(jnp.float32) * conv_in[tap_index : tap_index + seq_len]
        )
    activated = jax.nn.silu(convolved).astype(jnp.bfloat16)
    x_values = activated[:, :, :P_SIZE].astype(jnp.float32)
    group_span = lax.axis_size("head") // G
    my_index = lax.axis_index("head")
    own_maps = activated[:, :, P_SIZE:]
    for bit_number in range(group_span.bit_length() - 1):
        partner_maps = from_partner(own_maps, "head", bit_number)
        upper_half = my_index // (1 << bit_number) % 2 == 1
        own_maps = jnp.where(
            upper_half,
            jnp.concatenate([partner_maps, own_maps], axis=1),
            jnp.concatenate([own_maps, partner_maps], axis=1),
        )
    group_heads = own_maps.shape[1]
    slice_len = own_maps.shape[2] // 2
    group_index = my_index // group_span
    b_matrix = own_maps[:, :, :slice_len].reshape(seq_len, -1).astype(jnp.float32)
    c_matrix = own_maps[:, :, slice_len:].reshape(seq_len, -1).astype(jnp.float32)
    dt_vals = jax.nn.softplus(dt_raw + dt_bias)
    decay_rate = -jnp.exp(a_log)
    outputs, final_state = stretch_scan(
        x_values, dt_vals, decay_rate, b_matrix, c_matrix, init_state
    )
    outputs = outputs + d_skip[None, :, None] * x_values
    gated_out = outputs * jax.nn.silu(projected[:, :, :P_SIZE].astype(jnp.float32))
    own_sq = jnp.sum(gated_out * gated_out, axis=(1, 2))
    selector = (jnp.arange(G) == group_index).astype(jnp.float32)
    group_sq = lax.psum(own_sq[:, None] * selector[None, :], "head")
    chosen_sq = jnp.sum(group_sq * selector[None, :], axis=1)
    inverse = lax.rsqrt(chosen_sq / (P_SIZE * group_heads) + epsilon)
    normed_out = (gated_out * inverse[:, None, None] * norm_gain.astype(jnp.float32)).astype(
        jnp.bfloat16
    )
    normed_flat = normed_out.reshape(seq_len, -1)
    w_out_flat = w_out.reshape(-1, w_out.shape[2])
    summed = lax.psum_scatter(
        lax.dot_general(
            w_out_flat, normed_flat, (((0,), (1,)), ((), ())), preferred_element_type=jnp.float32
        ),
        "head",
        scatter_dimension=0,
        tiled=True,
    )
    mixer_out = summed.T.astype(jnp.bfloat16)
    return (mixer_out, final_state)


def solution(mesh):
    return jax.shard_map(
        per_device,
        mesh=mesh,
        in_specs=(
            P("parts", "head"),
            P("head"),
            P("head", None, None),
            P("head", None),
            P("head"),
            P("head"),
            P(None, "head", None),
            P("head", None),
            P("parts", "head", None),
            P(("parts", "head"), None, None),
            P("head"),
            P("head", None),
            P("head", None, None),
        ),
        out_specs=(P("parts", "head"), P(("parts", "head"), None, None)),
        check_vma=False,
    )
```

profile of v0, /device:TPU:0, one launch (start us, length us, event | category | flops | bytes accessed | tf_op | source)
XLA Modules:
  0.0 240.4 jit_solution(13922195646523875361)
XLA Ops:
  7.2 0.7 all-gather.3.cloned.1.call-update
  8.0 1.2 convert_element_type.66
  9.2 0.7 reshape.90
  9.9 0.7 convert_element_type.56
  10.5 23.2 %all-gather = bf16[16,1,512]{2,1,0:T(2,128)(2,1)S(1)} all-gather(bf16[1,1,512]{2,1,0:T(2,128)(2,1)S(1)} %reshape.90), channel_id=1, replica_groups=mesh['parts'=2,'head'=16] {'head'}, dimensions={0}, use_global_device_ids=true | all-gather | bytes 17408 | tf_op jit(solution)/shard_map/all_gather | solution.py:80
  33.8 0.8 copy.60
  35.9 0.7 bitcast_convert_fusion.3
  36.6 29.6 %all-gather.3.cloned.1.call-done = bf16[256,8192]{1,0:T(8,128)(2,1)} async-done(((bf16[256,512]{1,0:T(8,128)(2,1)}), bf16[256,8192]{1,0:T(8,128)(2,1)}) %all-gather.3.cloned.1.call-update) | async-done | bytes 4194320 | tf_op jit(solution)/shard_map/all_gather | solution.py:79
  66.2 3.1 %fusion.1 = f32[256]{0:T(256)S(1)} fusion(bf16[256,8192]{1,0:T(8,128)(2,1)} %all-gather.3.cloned.1.call-done), kind=kLoop, calls=%fused_computation.7 | loop fusion | flops 6291200 | bytes 4195328 | tf_op jit(solution)/shard_map/reduce_sum | solution.py:83
  69.3 3.5 %broadcast_multiply_fusion.1 = (f32[256,2]{0,1:T(2,128)S(1)}, f32[256,2]{0,1:T(2,128)S(1)}) fusion(f32[2]{0:T(128)S(1)} %exponential_negate_fusion, f32[2]{0:T(128)} %param.19, bf16[2,8192]{1,0:T(2,128)(2,1)} %param.18, bf16[256,8192]{1,0:T(8,128)(2,1)} %all-gather.3.cloned.1.call-done, f32[8192]{0:T(1024)S(1)} %bitcast.69, f32[256]{0:T(256)S(1)} %add_rsqrt_fusion.1), kind=kOutput, calls=%fused_computation.68 | convolution fusion | flops 16781312 | bytes 4264976 | tf_op jit(solution)/shard_map/dot_general | solution.py:86
  73.2 0.7 copy.64
  73.8 7.1 %convolution_convert_fusion = bf16[256,512]{1,0:T(8,128)(2,1)S(1)} fusion(bf16[512,8192]{1,0:T(8,128)(2,1)} %bitcast.74, bf16[256,8192]{1,0:T(8,128)(2,1)} %all-gather.3.cloned.1.call-done, f32[8192]{0:T(1024)S(1)} %bitcast.70, f32[256]{0:T(256)S(1)} %add_rsqrt_fusion.1), kind=kOutput, calls=%fused_computation.10 | convolution fusion | flops 2156003328 | bytes 12878848 | tf_op jit(solution)/shard_map/dot_general | solution.py:85
  83.8 1.0 collective-permute-done
  85.3 2.9 %while.12 = (s32[]{:T(128)}, f32[2,64,256]{2,1,0:T(8,128)S(1)}, f32[2,2,64,256]{3,2,1,0:T(8,128)}, f32[2,2]{1,0:T(2,128)}, f32[2,2,64,256]{3,2,1,0:T(8,128)S(1)}, /*index=5*/s32[]{:T(128)}) while((s32[]{:T(128)}, f32[2,64,256]{2,1,0:T(8,128)S(1)}, f32[2,2,64,256]{3,2,1,0:T(8,128)}, f32[2,2]{1,0:T(2,128)}, f32[2,2,64,256]{3,2,1,0:T(8,128)S(1)}, ...), condition=%wide.region_3.4_spmd, body=%wide.region_2.3_spmd.sunk | while | flops 65538 | bytes 655473 | solution.py:52
  85.3 0.7 fusion.55
  86.8 0.7 fusion.55
  88.5 1.2 convolution_bitcast_fusion.1
  89.7 1.2 fusion.8
  90.9 0.8 multiply_reduce_fusion
  92.4 31.4 %psum.7 = f32[256,8]{0,1:T(8,128)S(1)} all-reduce(f32[256,8]{0,1:T(8,128)S(1)} %broadcast_multiply_fusion), channel_id=1, replica_groups=mesh['parts'=2,'head'=16] {'head'}, use_global_device_ids=true, to_apply=%region_5.6 | all-reduce | flops 2048 | bytes 16384 | tf_op jit(solution)/shard_map/psum | solution.py:122
  123.8 0.7 multiply_reduce_fusion.1
  124.5 5.2 %convolution_bitcast_fusion = f32[8192,256]{0,1:T(8,128)} fusion(bf16[2,64,8192]{2,1,0:T(8,128)(2,1)S(1)} %copy-done, f32[256,2,64]{0,2,1:T(8,128)S(1)} %get-tuple-element.43, f32[2,64]{1,0:T(2,128)} %convert_element_type.66, f32[256]{0:T(256)S(1)} %add_rsqrt_fusion), kind=kOutput, calls=%fused_computation.4 | convolution fusion | flops 536969216 | bytes 10618368 | tf_op jit(solution)/shard_map/dot_general | solution.py:131
  129.7 102.1 %reduce-scatter.2.cloned.1.call-done = f32[512,256]{0,1:T(8,128)} async-done(((f32[8192,256]{0,1:T(8,128)}), f32[512,256]{0,1:T(8,128)}) %reduce-scatter.2.cloned.1.call-update) | async-done | bytes 524304 | tf_op jit(solution)/shard_map/reduce_scatter | solution.py:130
  231.8 1.8 convert_bitcast_fusion
  (46 shorter events, 7.3 us)
Async XLA Ops:
  7.2 117.3 %copy-start = (bf16[2,64,8192]{2,1,0:T(8,128)(2,1)S(1)}, bf16[2,64,8192]{2,1,0:T(8,128)(2,1)}, u32[]{:S(2)}) copy-start(bf16[2,64,8192]{2,1,0:T(8,128)(2,1)} %param.27) | copy-start | bytes 6291460
  7.2 59.0 %all-gather.3.cloned.1.call-start = ((), (), s32[]{:S(2)}) async-start(), calls=%async_computation.1 | async-start | bytes 4456448 | tf_op jit(solution)/shard_map/all_gather | solution.py:79
  7.9 223.8 %reduce-scatter.2.cloned.1.call-start = ((), (), s32[]{:S(2)}) async-start(), calls=%async_computation.2 | async-start | bytes 8912896 | tf_op jit(solution)/shard_map/reduce_scatter | solution.py:130
  72.8 9.7 %copy-start.3 = (f32[256,2]{0,1:T(2,128)}, f32[256,2]{0,1:T(2,128)S(1)}, u32[]{:S(2)}) copy-start(f32[256,2]{0,1:T(2,128)S(1)} %get-tuple-element.55) | copy-start | bytes 6148
  73.8 11.5 %copy-start.2 = (f32[2,64,256]{2,1,0:T(8,128)S(1)}, f32[2,64,256]{2,1,0:T(8,128)}, u32[]{:S(2)}) copy-start(f32[2,64,256]{2,1,0:T(8,128)} %param.24) | copy-start | bytes 393220
  83.5 1.4 collective-permute-start
  88.2 41.4 %copy-start.1 = (f32[2,64,256]{2,1,0:T(8,128)}, f32[2,64,256]{2,1,0:T(8,128)S(1)}, u32[]{:S(2)}) copy-start(f32[2,64,256]{2,1,0:T(8,128)S(1)} %get-tuple-element.29) | copy-start | bytes 393220
Sparse Core Ops, SparseCore 0:
  10.2 55.9 all-gather.2
  129.8 101.9 reduce-scatter.1
where the time goes:
time: 241 us; the launch traced here: 240 us
  waiting for transfers between devices  133 us (55%)
  blocking collectives  54.6 us (23%)
  matrix products  18.7 us (8%)
  between operations  14.3 us (6%)
  other arithmetic  12.1 us (5%)
  local copies, waits for them, and re-layouts  6.8 us (3%)
    reduce_scatter x1, waiting for transfers between devices, per_device(): lax.psum_scatter(lax.dot_general(w_out_flat, normed_flat, (((0,), (1,)),...  102 us
    psum x1, blocking collectives, per_device(): group_sq = lax.psum(own_sq[:, None] * selector[None, :], 'head')  31.4 us
    all_gather x1, waiting for transfers between devices, per_device(): lax.all_gather(tokens, 'head', axis=1, tiled=True)  29.6 us
    all_gather x1, blocking collectives, per_device(): lax.all_gather(pre_gain, 'head', axis=0, tiled=True)  23.2 us
    dot_general x1, matrix products, per_device(): lax.dot_general(normed_in, w_flat, contract_last, preferred_element_type=...  7.05 us
    dot_general x1, matrix products, per_device(): lax.dot_general(w_out_flat, normed_flat, (((0,), (1,)), ((), ())), prefer...  5.17 us
  transfers between devices with their start and end apart: 3, of which 3 were waited for; matrix products, arithmetic and copies ran while one was open for 2% of the time, Pallas kernels for 0%

commit v1 on v0

--- a/solution.py
+++ b/solution.py
@@ -18,6 +18,12 @@
         if high != low and high < count:
             route += [(low, high), (high, low)]
     return lax.ppermute(block, axis, route)
+
+
+def halves(values):
+    high = values.astype(jnp.bfloat16)
+    low = (values - lax.reduce_precision(values, 8, 7)).astype(jnp.bfloat16)
+    return high, low
 
 
 def stretch_scan(x_values, dt_vals, decay_rate, b_matrix, c_matrix, start_state):
@@ -75,15 +81,30 @@
     width_full = w_in.shape[2]
     w_flat = w_in.reshape(-1, width_full)
     contract_last = (((1,), (1,)), ((), ()))
-    rows_full, gain_full = (
-        lax.all_gather(tokens, "head", axis=1, tiled=True),
-        lax.all_gather(pre_gain, "head", axis=0, tiled=True),
+    w_out_flat = w_out.reshape(-1, w_out.shape[2])
+    w_columns = lax.all_to_all(w_out_flat, "head", split_axis=1, concat_axis=0, tiled=True)
+    wide_tokens = tokens.astype(jnp.float32)
+    gained = (wide_tokens * pre_gain.astype(jnp.float32)).astype(jnp.bfloat16)
+    block_width = tokens.shape[1]
+    shard_count = lax.axis_size("head")
+    block_sq = jnp.sum(wide_tokens * wide_tokens, axis=1)
+    sq_parts = jnp.stack(halves(block_sq)).reshape(-1)
+    sq_rows = -(-sq_parts.shape[0] // block_width)
+    sq_rows = -(-sq_rows // 16) * 16
+    sq_block = jnp.pad(sq_parts, (0, sq_rows * block_width - sq_parts.shape[0]))
+    payload = jnp.concatenate([gained, sq_block.reshape(sq_rows, block_width)], axis=0)
+    gathered = lax.all_gather(payload, "head", axis=1, tiled=True)
+    sq_all = gathered[seq_len:].astype(jnp.float32).reshape(sq_rows, shard_count, block_width)
+    sq_all = jnp.sum(sq_all, axis=1).reshape(-1)
+    row_sq = sq_all[:seq_len] + sq_all[seq_len : 2 * seq_len]
+    row_scale = lax.rsqrt(row_sq / width_full + epsilon)[:, None]
+    gained_full = gathered[:seq_len]
+    proj_sum = row_scale * lax.dot_general(
+        gained_full, w_flat, contract_last, preferred_element_type=jnp.float32
     )
-    wide_tokens = rows_full.astype(jnp.float32)
-    row_scale = lax.rsqrt(jnp.mean(wide_tokens * wide_tokens, axis=1, keepdims=True) + epsilon)
-    normed_in = (wide_tokens * row_scale * gain_full.astype(jnp.float32)).astype(jnp.bfloat16)
-    proj_sum = lax.dot_general(normed_in, w_flat, contract_last, preferred_element_type=jnp.float32)
-    dt_raw = lax.dot_general(normed_in, w_dt, contract_last, preferred_element_type=jnp.float32)
+    dt_raw = row_scale * lax.dot_general(
+        gained_full, w_dt, contract_last, preferred_element_type=jnp.float32
+    )
     projected = proj_sum.astype(jnp.bfloat16).reshape(seq_len, heads_here, -1)
     conv_in = jnp.concatenate([conv_tail, projected[:, :, P_SIZE:]], axis=0).astype(jnp.float32)
     convolved = jnp.zeros((seq_len,) + conv_bias.shape, jnp.float32) + conv_bias.astype(jnp.float32)
@@ -107,7 +128,6 @@
         )
     group_heads = own_maps.shape[1]
     slice_len = own_maps.shape[2] // 2
-    group_index = my_index // group_span
     b_matrix = own_maps[:, :, :slice_len].reshape(seq_len, -1).astype(jnp.float32)
     c_matrix = own_maps[:, :, slice_len:].reshape(seq_len, -1).astype(jnp.float32)
     dt_vals = jax.nn.softplus(dt_raw + dt_bias)
@@ -117,25 +137,23 @@
     )
     outputs = outputs + d_skip[None, :, None] * x_values
     gated_out = outputs * jax.nn.silu(projected[:, :, :P_SIZE].astype(jnp.float32))
-    own_sq = jnp.sum(gated_out * gated_out, axis=(1, 2))
-    selector = (jnp.arange(G) == group_index).astype(jnp.float32)
-    group_sq = lax.psum(own_sq[:, None] * selector[None, :], "head")
-    chosen_sq = jnp.sum(group_sq * selector[None, :], axis=1)
-    inverse = lax.rsqrt(chosen_sq / (P_SIZE * group_heads) + epsilon)
-    normed_out = (gated_out * inverse[:, None, None] * norm_gain.astype(jnp.float32)).astype(
-        jnp.bfloat16
+    own_width = heads_here * P_SIZE
+    gated_rows = jnp.concatenate(
+        [
+            gated_out.reshape(seq_len, own_width).astype(jnp.bfloat16),
+            jnp.broadcast_to(norm_gain.reshape(1, own_width), (16, own_width)),
+        ],
+        axis=0,
     )
-    normed_flat = normed_out.reshape(seq_len, -1)
-    w_out_flat = w_out.reshape(-1, w_out.shape[2])
-    summed = lax.psum_scatter(
-        lax.dot_general(
-            w_out_flat, normed_flat, (((0,), (1,)), ((), ())), preferred_element_type=jnp.float32
-        ),
-        "head",
-        scatter_dimension=0,
-        tiled=True,
-    )
-    mixer_out = summed.T.astype(jnp.bfloat16)
+    gated_full = lax.all_gather(gated_rows, "head", axis=1, tiled=True).astype(jnp.float32)
+    gains = gated_full[seq_len].reshape(G, -1)
+    gated_groups = gated_full[:seq_len].reshape(seq_len, G, -1)
+    group_sq = jnp.sum(gated_groups * gated_groups, axis=2, keepdims=True)
+    inverse = lax.rsqrt(group_sq / (P_SIZE * group_heads) + epsilon)
+    normed_out = (gated_groups * inverse * gains[None]).astype(jnp.bfloat16)
+    mixer_out = jnp.dot(
+        normed_out.reshape(seq_len, -1), w_columns, preferred_element_type=jnp.float32
+    ).astype(jnp.bfloat16)
     return (mixer_out, final_state)
 
 

time: 241 us -> 172 us (0.71)
  blocking collectives: 54.6 us -> 0 us
  waiting for transfers between devices: 133 us -> 114 us
  starting transfers between devices: 0.4 us -> 7.89 us
  matrix products: 18.7 us -> 16.2 us
    reduce_scatter x1 -> x0, waiting for transfers between devices: 102 us -> none  [per_device(): lax.psum_scatter(lax.dot_general(w_out_flat, normed_flat, (((0,), (1,)),...]
    all_gather x1 -> x2, waiting for transfers between devices: 29.6 us -> 113 us  [the longest x1 76.3 us: per_device(): gathered = lax.all_gather(payload, 'head', axis=1, tiled=True)]
    psum x1 -> x0, blocking collectives: 31.4 us -> none  [per_device(): group_sq = lax.psum(own_sq[:, None] * selector[None, :], 'head')]
    all_gather x1 -> x0, blocking collectives: 23.2 us -> none  [per_device(): lax.all_gather(pre_gain, 'head', axis=0, tiled=True)]
    all_to_all x0 -> x1, starting transfers between devices: none -> 7.5 us  [per_device(): lax.all_to_all(w_out_flat, 'head', split_axis=1, concat_axis=0, tiled=True)]
    reduce_sum x3 -> x2, other arithmetic: 4.55 us -> 0.23 us  [the longest x1 0.15 us: per_device(): group_sq = jnp.sum(gated_groups * gated_groups, axis=2, keepdims=True)]
    dot_general x3, matrix products: 15.7 us -> 13.1 us  [the longest x1 7.02 us: per_device(): lax.dot_general(gained_full, w_flat, contract_last, preferred_element_typ...]
    all_to_all x0 -> x1, local copies, waits for them, and re-layouts: none -> 2.52 us  [per_device(): lax.all_to_all(w_out_flat, 'head', split_axis=1, concat_axis=0, tiled=True)]
  transfers between devices with their start and end apart: 3 -> 4, of which waited for: 3 -> 3; matrix products, arithmetic and copies ran while one was open for 2% -> 17% of each run, Pallas kernels for 0% -> 0%
where the time goes in v1:
time: 172 us; the launch traced here: 171 us
  waiting for transfers between devices  114 us (66%)
  matrix products  16.2 us (9%)
  between operations  14.5 us (8%)
  other arithmetic  9.79 us (6%)
  local copies, waits for them, and re-layouts  8.8 us (5%)
  starting transfers between devices  7.89 us (5%)
    all_gather x1, waiting for transfers between devices, per_device(): gathered = lax.all_gather(payload, 'head', axis=1, tiled=True)  76.3 us
    all_gather x1, waiting for transfers between devices, per_device(): lax.all_gather(gated_rows, 'head', axis=1, tiled=True).astype(jnp.float32)  37 us
    all_to_all x1, starting transfers between devices, per_device(): lax.all_to_all(w_out_flat, 'head', split_axis=1, concat_axis=0, tiled=True)  7.5 us
    dot_general x1, matrix products, per_device(): lax.dot_general(gained_full, w_flat, contract_last, preferred_element_typ...  7.02 us
  transfers between devices with their start and end apart: 4, of which 3 were waited for; matrix products, arithmetic and copies ran while one was open for 17% of the time, Pallas kernels for 0%

profile of v1, /device:TPU:0, one launch (start us, length us, event | category | flops | bytes accessed | tf_op | source)
XLA Modules:
  0.0 171.3 jit_solution(12366358647404050358)
XLA Ops:
  7.2 0.7 convert_element_type.78
  7.9 1.1 fusion.21
  9.1 0.7 pad_maximum_fusion
  9.9 2.4 %copy.87 = bf16[16,8,16,512]{3,2,1,0:T(8,128)(2,1)S(1)} copy(bf16[16,8,16,512]{3,1,2,0:T(8,128)(2,1)} %bitcast.83) | data formatting | bytes 4194304
  12.3 2.5 %copy.72 = bf16[128,16,512]{2,0,1:T(8,128)(2,1)} copy(bf16[128,16,512]{2,1,0:T(8,128)(2,1)S(1)} %bitcast.82) | data formatting | bytes 4194304 | tf_op jit(solution)/shard_map/all_to_all | solution.py:85
  14.8 7.5 %all-to-all-start = ((bf16[128,16,512]{2,0,1:T(8,128)(2,1)}), bf16[128,16,512]{2,0,1:T(8,128)(2,1)S(1)}, u32[]{:S(2)}, u32[]{:S(2)}) async-start(bf16[128,16,512]{2,0,1:T(8,128)(2,1)} %copy.72), calls=%async_computation | async-start | bytes 4194304 | tf_op jit(solution)/shard_map/all_to_all | solution.py:85
  22.8 76.3 %all-gather.3.cloned.1.call-done = bf16[272,8192]{1,0:T(8,128)(2,1)} async-done(((bf16[272,512]{1,0:T(8,128)(2,1)}), bf16[272,8192]{1,0:T(8,128)(2,1)}) %all-gather.3.cloned.1.call-update) | async-done | bytes 4456464 | tf_op jit(solution)/shard_map/all_gather | solution.py:96
  99.1 1.0 slice_convert_fusion
  100.5 7.0 %fusion.10 = bf16[256,512]{1,0:T(8,128)(2,1)S(1)} fusion(bf16[512,8192]{1,0:T(8,128)(2,1)} %bitcast.101, bf16[272,8192]{1,0:T(8,128)(2,1)} %all-gather.3.cloned.1.call-done, f32[256]{0:T(256)S(1)} %fusion.58), kind=kOutput, calls=%fused_computation.14 | convolution fusion | flops 2147745792 | bytes 12846080 | tf_op jit(solution)/shard_map/dot_general | solution.py:102
  107.9 0.7 multiply_convert_fusion
  108.6 0.6 fusion.61
  109.2 3.4 %broadcast_multiply_fusion = (f32[256,2]{0,1:T(2,128)S(1)}, f32[256,2]{0,1:T(2,128)S(1)}) fusion(f32[2]{0:T(128)S(1)} %exponential_negate_fusion, f32[2]{0:T(128)S(1)} %copy-done.9, bf16[2,8192]{1,0:T(2,128)(2,1)S(1)} %copy-done, bf16[272,8192]{1,0:T(8,128)(2,1)} %all-gather.3.cloned.1.call-done, f32[256]{0:T(256)S(1)} %fusion.58), kind=kOutput, calls=%fused_computation.77 | convolution fusion | flops 8393216 | bytes 4232208 | tf_op jit(solution)/shard_map/dot_general | solution.py:105
  113.8 0.8 collective-permute-done
  114.6 1.0 maximum_select_fusion
  116.2 1.3 convolution_bitcast_fusion
  117.6 1.6 while.12
  117.6 0.7 bitcast_dynamic-update-slice_fusion.2
  118.4 0.7 bitcast_dynamic-update-slice_fusion.2
  119.2 1.3 fusion.14
  120.6 0.7 pad_maximum_fusion.1
  121.3 37.0 %all-gather.5.cloned.1.call-done = bf16[272,2048]{0,1:T(8,128)(2,1)} async-done(((bf16[272,128]{0,1:T(8,128)(2,1)}), bf16[272,2048]{0,1:T(8,128)(2,1)}) %all-gather.5.cloned.1.call-update) | async-done | bytes 1114128 | tf_op jit(solution)/shard_map/all_gather | solution.py:148
  158.3 1.6 convert_element_type.89
  160.5 1.3 fusion.6
  161.8 2.7 %convolution_convert_fusion = bf16[256,512]{1,0:T(8,128)(2,1)} fusion(bf16[256,2048]{0,1:T(8,128)(2,1)} %fusion.6, bf16[2048,512]{1,0:T(8,128)(2,1)S(1)} %bitcast.84), kind=kOutput, calls=%fused_computation.15 | convolution fusion | flops 537001984 | bytes 3407872 | tf_op jit(solution)/shard_map/dot_general | solution.py:154
  (72 shorter events, 3.8 us)
Async XLA Ops:
  7.2 102.1 %copy-start = (bf16[2,8192]{1,0:T(2,128)(2,1)S(1)}, bf16[2,8192]{1,0:T(2,128)(2,1)}, u32[]{:S(2)}) copy-start(bf16[2,8192]{1,0:T(2,128)(2,1)} %param.18) | copy-start | bytes 98308
  7.2 91.9 %all-gather.3.cloned.1.call-start = ((), (), s32[]{:S(2)}) async-start(), calls=%async_computation.1 | async-start | bytes 4734976 | tf_op jit(solution)/shard_map/all_gather | solution.py:96
  14.8 7.6 %copy-start.7 = (bf16[2,64]{1,0:T(2,128)(2,1)S(1)}, bf16[2,64]{1,0:T(2,128)(2,1)}, u32[]{:S(2)}) copy-start(bf16[2,64]{1,0:T(2,128)(2,1)} %param.26) | copy-start | bytes 772
  14.8 7.7 %copy-start.4 = (bf16[3,2,192]{2,1,0:T(2,128)(2,1)S(1)}, bf16[3,2,192]{2,1,0:T(2,128)(2,1)}, u32[]{:S(2)}) copy-start(bf16[3,2,192]{2,1,0:T(2,128)(2,1)} %param.23) | copy-start | bytes 6916
  14.8 7.9 %copy-start.5 = (bf16[2,192]{1,0:T(2,128)(2,1)S(1)}, bf16[2,192]{1,0:T(2,128)(2,1)}, u32[]{:S(2)}) copy-start(bf16[2,192]{1,0:T(2,128)(2,1)} %param.22) | copy-start | bytes 2308
  14.8 7.9 %copy-start.8 = (f32[2]{0:T(128)S(1)}, f32[2]{0:T(128)}, u32[]{:S(2)}) copy-start(f32[2]{0:T(128)} %param.20) | copy-start | bytes 28
  14.8 7.9 %copy-start.3 = (bf16[4,2,192]{2,1,0:T(2,128)(2,1)S(1)}, bf16[4,2,192]{2,1,0:T(2,128)(2,1)}, u32[]{:S(2)}) copy-start(bf16[4,2,192]{2,1,0:T(2,128)(2,1)} %param.21) | copy-start | bytes 9220
  14.8 147.0 %all-to-all-start = ((bf16[128,16,512]{2,0,1:T(8,128)(2,1)}), bf16[128,16,512]{2,0,1:T(8,128)(2,1)S(1)}, u32[]{:S(2)}, u32[]{:S(2)}) async-start(bf16[128,16,512]{2,0,1:T(8,128)(2,1)} %copy.72), calls=%async_computation | async-start | bytes 4194304 | tf_op jit(solution)/shard_map/all_to_all | solution.py:85
  22.3 136.0 %all-gather.5.cloned.1.call-start = ((), (), s32[]{:S(2)}) async-start(), calls=%async_computation.2 | async-start | bytes 1671168 | tf_op jit(solution)/shard_map/all_gather | solution.py:148
  107.5 1.7 copy-start.9
  112.6 4.9 %copy-start.2 = (f32[2,64,256]{2,1,0:T(8,128)S(1)}, f32[2,64,256]{2,1,0:T(8,128)}, u32[]{:S(2)}) copy-start(f32[2,64,256]{2,1,0:T(8,128)} %param.24) | copy-start | bytes 393220
  113.1 1.5 collective-permute-start
  115.6 4.8 %copy-start.6 = (f32[2]{0:T(128)S(1)}, f32[2]{0:T(128)}, u32[]{:S(2)}) copy-start(f32[2]{0:T(128)} %param.25) | copy-start | bytes 28
  119.1 41.2 %copy-start.1 = (f32[2,64,256]{2,1,0:T(8,128)}, f32[2,64,256]{2,1,0:T(8,128)S(1)}, u32[]{:S(2)}) copy-start(f32[2,64,256]{2,1,0:T(8,128)S(1)} %get-tuple-element.29) | copy-start | bytes 393220
Sparse Core Ops, SparseCore 0:
  10.2 88.8 all-gather.2
  121.4 36.8 all-gather.4

commit v2 on v1

--- a/solution.py
+++ b/solution.py
@@ -1,6 +1,10 @@
+import functools
+
 import jax
 import jax.numpy as jnp
 from jax import lax
+from jax.experimental import pallas as pl
+from jax.experimental.pallas import tpu as pltpu
 from jax.sharding import PartitionSpec as P
 
 P_SIZE = 64
@@ -18,6 +22,110 @@
         if high != low and high < count:
             route += [(low, high), (high, low)]
     return lax.ppermute(block, axis, route)
+
+
+def spread(depth, own_ref, full_ref, local_sem, send_sem, recv_sem):
+    me = lax.axis_index("head")
+    row, column, core = me // 4, (me // 2) % 2, me % 2
+    width = own_ref.shape[1]
+    across, beside = me + 2 - 4 * column, me + 1 - 2 * core
+    has_upper, has_lower = row < depth - 1, row > 0
+
+    def place(block):
+        return full_ref.at[:, pl.ds(pl.multiple_of(block * width, 128), width)]
+
+    def copy(block, way, target, source=None):
+        return pltpu.make_async_remote_copy(
+            src_ref=place(block) if source is None else source,
+            dst_ref=place(block),
+            send_sem=send_sem.at[way, block],
+            recv_sem=recv_sem.at[block],
+            device_id={"head": target},
+            device_id_type=pl.DeviceIdType.MESH,
+        )
+
+    def arrived(block):
+        copy(block, 3, beside).wait_recv()
+
+    barrier = pltpu.get_barrier_semaphore()
+
+    def greet(target):
+        pl.semaphore_signal(
+            barrier, inc=1, device_id={"head": target}, device_id_type=pl.DeviceIdType.MESH
+        )
+
+    greet(across)
+    greet(beside)
+    pl.when(has_upper)(lambda: greet(me + 4))
+    pl.when(has_lower)(lambda: greet(me - 4))
+    neighbours = 2 + has_upper.astype(jnp.int32) + has_lower.astype(jnp.int32)
+    pl.semaphore_wait(barrier, neighbours)
+
+    pl.when(has_upper)(lambda: copy(me, 0, me + 4, own_ref).start())
+    pl.when(has_lower)(lambda: copy(me, 1, me - 4, own_ref).start())
+    copy(me, 2, across, own_ref).start()
+    copy(me, 3, beside, own_ref).start()
+    keep = pltpu.make_async_copy(own_ref, place(me), local_sem)
+    keep.start()
+
+    def relay(block):
+        arrived(block)
+        copy(block, 3, beside).start()
+
+    def from_lower(block):
+        arrived(block)
+        pl.when(has_upper)(lambda: copy(block, 0, me + 4).start())
+        copy(block, 2, across).start()
+        copy(block, 3, beside).start()
+
+    def from_upper(block):
+        arrived(block)
+        pl.when(has_lower)(lambda: copy(block, 1, me - 4).start())
+        copy(block, 2, across).start()
+        copy(block, 3, beside).start()
+
+    relay(across)
+    for apart in range(1, depth):
+        below, above = row - apart >= 0, row + apart < depth
+        pl.when(below)(lambda: from_lower(me - 4 * apart))
+        pl.when(above)(lambda: from_upper(me + 4 * apart))
+        pl.when(below)(lambda: relay(across - 4 * apart))
+        pl.when(above)(lambda: relay(across + 4 * apart))
+
+    for level in range(depth):
+        for side in range(2):
+            arrived(level * 4 + side * 2 + 1 - core)
+    for level in range(depth):
+        own = level * 4 + column * 2 + core
+        other = level * 4 + (1 - column) * 2 + core
+        pl.when(has_upper & (level <= row))(lambda: copy(own, 0, me + 4, own_ref).wait_send())
+        pl.when(has_lower & (level >= row))(lambda: copy(own, 1, me - 4, own_ref).wait_send())
+        copy(own, 2, across, own_ref).wait_send()
+        copy(own, 3, beside, own_ref).wait_send()
+        copy(other, 3, beside, own_ref).wait_send()
+    keep.wait()
+
+
+def gather_columns(block, number):
+    count = lax.axis_size("head")
+    rows, width = block.shape
+    if width % 128 or count % 4 or count > 16:
+        return lax.all_gather(block, "head", axis=1, tiled=True)
+    return pl.pallas_call(
+        functools.partial(spread, count // 4),
+        out_shape=jax.ShapeDtypeStruct((rows, width * count), block.dtype),
+        in_specs=[pl.BlockSpec(memory_space=pl.ANY)],
+        out_specs=pl.BlockSpec(memory_space=pl.ANY),
+        scratch_shapes=[
+            pltpu.SemaphoreType.DMA,
+            pltpu.SemaphoreType.DMA((4, count)),
+            pltpu.SemaphoreType.DMA((count,)),
+        ],
+        compiler_params=pltpu.CompilerParams(collective_id=number, has_side_effects=True),
+        cost_estimate=pl.CostEstimate(
+            flops=0, bytes_accessed=rows * width * count * 16, transcendentals=0
+        ),
+    )(block)
 
 
 def halves(values):
@@ -93,7 +201,7 @@
     sq_rows = -(-sq_rows // 16) * 16
     sq_block = jnp.pad(sq_parts, (0, sq_rows * block_width - sq_parts.shape[0]))
     payload = jnp.concatenate([gained, sq_block.reshape(sq_rows, block_width)], axis=0)
-    gathered = lax.all_gather(payload, "head", axis=1, tiled=True)
+    gathered = gather_columns(payload, 1)
     sq_all = gathered[seq_len:].astype(jnp.float32).reshape(sq_rows, shard_count, block_width)
     sq_all = jnp.sum(sq_all, axis=1).reshape(-1)
     row_sq = sq_all[:seq_len] + sq_all[seq_len : 2 * seq_len]
@@ -145,7 +253,7 @@
         ],
         axis=0,
     )
-    gated_full = lax.all_gather(gated_rows, "head", axis=1, tiled=True).astype(jnp.float32)
+    gated_full = gather_columns(gated_rows, 2).astype(jnp.float32)
     gains = gated_full[seq_len].reshape(G, -1)
     gated_groups = gated_full[:seq_len].reshape(seq_len, G, -1)
     group_sq = jnp.sum(gated_groups * gated_groups, axis=2, keepdims=True)

time: 172 us -> 144 us (0.84)
  waiting for transfers between devices: 114 us -> 0.01 us
  Pallas kernels: 0 us -> 99.4 us
  between operations: 14.5 us -> 1.14 us
  local copies, waits for them, and re-layouts: 8.8 us -> 12.4 us
  other arithmetic: 9.79 us -> 7.73 us
    all_gather x2 -> x0, waiting for transfers between devices: 113 us -> none  [the longest x1 76.3 us: per_device(): gathered = lax.all_gather(payload, 'head', axis=1, tiled=True)]
    pallas_call x0 -> x2, Pallas kernels: none -> 99.4 us  [gather_columns(): pl.pallas_call(functools.partial(spread, count // 4), out_shape=jax.Shape...]
    unnamed x25 -> x31, local copies, waits for them, and re-layouts: 2.97 us -> 7.46 us
    reduce_sum x1, other arithmetic: 0.15 us -> 1.94 us  [per_device(): group_sq = jnp.sum(gated_groups * gated_groups, axis=2, keepdims=True)]
  transfers between devices with their start and end apart: 4 -> 2, of which waited for: 3 -> 0; matrix products, arithmetic and copies ran while one was open for 17% -> 19% of each run, Pallas kernels for 0% -> 69%
where the time goes in v2:
time: 144 us
  Pallas kernels  99.4 us (69%)
  matrix products  15.3 us (11%)
  local copies, waits for them, and re-layouts  12.4 us (9%)
  starting transfers between devices  8.01 us (6%)
  other arithmetic  7.73 us (5%)
    pallas_call x2, Pallas kernels, gather_columns(): pl.pallas_call(functools.partial(spread, count // 4), out_shape=jax.Shape...  99.4 us
    all_to_all x1, starting transfers between devices, per_device(): lax.all_to_all(w_out_flat, 'head', split_axis=1, concat_axis=0, tiled=True)  7.55 us
    unnamed x31, local copies, waits for them, and re-layouts  7.46 us
    dot_general x1, matrix products, per_device(): lax.dot_general(gained_full, w_flat, contract_last, preferred_element_typ...  7.02 us
    dot_general x1, matrix products, per_device(): jnp.dot(normed_out.reshape(seq_len, -1), w_columns, preferred_element_typ...  3.63 us
    dot_general x1, matrix products, per_device(): lax.dot_general(gained_full, w_dt, contract_last, preferred_element_type=...  3.4 us
  transfers between devices with their start and end apart: 2, of which 0 were waited for; matrix products, arithmetic and copies ran while one was open for 19% of the time, Pallas kernels for 69%

profile of v2, /device:TPU:0, one launch (start us, length us, event | category | flops | bytes accessed | tf_op | source)
XLA Modules:
  0.0 144.0 jit_solution(12046870713861069531)
XLA Ops:
  0.6 2.4 %copy.133 = bf16[16,8,16,512]{3,2,1,0:T(8,128)(2,1)S(1)} copy(bf16[16,8,16,512]{3,1,2,0:T(8,128)(2,1)} %bitcast.83) | data formatting | bytes 4194304
  3.1 2.6 %copy.116 = bf16[128,16,512]{2,0,1:T(8,128)(2,1)} copy(bf16[128,16,512]{2,1,0:T(8,128)(2,1)S(1)} %bitcast.81) | data formatting | bytes 4194304 | tf_op jit(solution)/shard_map/all_to_all | solution.py:193
  5.7 7.6 %all-to-all-start = ((bf16[128,16,512]{2,0,1:T(8,128)(2,1)}), bf16[128,16,512]{2,0,1:T(8,128)(2,1)}, u32[]{:S(2)}, u32[]{:S(2)}) async-start(bf16[128,16,512]{2,0,1:T(8,128)(2,1)} %copy.116), calls=%async_computation | async-start | bytes 4194304 | tf_op jit(solution)/shard_map/all_to_all | solution.py:193
  13.7 0.7 pad_maximum_fusion.own_ref
  14.5 77.3 %shard_map.140 = bf16[272,8192]{1,0:T(8,128)(2,1)} custom-call(bf16[272,512]{1,0:T(8,128)(2,1)} %pad_maximum_fusion.own_ref), custom_call_target="tpu_custom_call" | custom-call | bytes 35651584 | tf_op jit(solution)/shard_map/pallas_call | solution.py:114
  91.7 1.0 slice_convert_fusion
  92.7 0.3 copy.129
  93.2 7.0 %fusion.8 = bf16[256,512]{1,0:T(8,128)(2,1)S(1)} fusion(bf16[512,8192]{1,0:T(8,128)(2,1)} %bitcast.101, bf16[272,8192]{1,0:T(8,128)(2,1)} %shard_map.140, f32[256]{0:T(256)S(1)} %fusion.57), kind=kOutput, calls=%fused_computation.11 | convolution fusion | flops 2147745792 | bytes 12846080 | tf_op jit(solution)/shard_map/dot_general | solution.py:210
  100.6 0.7 multiply_convert_fusion.2
  101.2 0.5 collective-permute-start
  101.7 3.4 %broadcast_multiply_fusion = (f32[256,2]{0,1:T(2,128)S(1)}, f32[256,2]{0,1:T(2,128)S(1)}) fusion(f32[2]{0:T(128)S(1)} %exponential_negate_fusion, f32[2]{0:T(128)S(1)} %copy-done.10, bf16[2,8192]{1,0:T(2,128)(2,1)S(1)} %copy-done, bf16[272,8192]{1,0:T(8,128)(2,1)} %shard_map.140, f32[256]{0:T(256)S(1)} %fusion.57), kind=kOutput, calls=%fused_computation.74 | convolution fusion | flops 8393216 | bytes 4232208 | tf_op jit(solution)/shard_map/dot_general | solution.py:213
  106.6 0.5 convolution_bitcast_fusion
  107.1 0.3 fusion.36
  107.4 0.3 while.12
  107.7 0.3 fusion.12
  108.2 0.6 pad_maximum_fusion.1.own_ref
  108.9 22.1 %shard_map.141 = bf16[272,2048]{1,0:T(8,128)(2,1)} custom-call(bf16[272,128]{1,0:T(8,128)(2,1)} %pad_maximum_fusion.1.own_ref), custom_call_target="tpu_custom_call" | custom-call | bytes 8912896 | tf_op jit(solution)/shard_map/pallas_call | solution.py:114
  131.0 0.8 slice.99
  131.8 1.5 %convert_element_type.89 = f32[272,2048]{1,0:T(8,128)S(1)} convert(bf16[272,2048]{1,0:T(8,128)(2,1)} %shard_map.141) | non-fusion elementwise | flops 557056 | bytes 3342336 | tf_op jit(solution)/shard_map/convert_element_type | solution.py:256
  133.5 2.2 %copy.131 = f32[32,8,8,256]{3,2,1,0:T(8,128)} copy(f32[32,8,8,256]{3,1,2,0:T(8,128)S(1)} %bitcast.82) | data formatting | bytes 4194304
  135.7 1.9 %reduce_sum.32 = f32[256,8]{1,0:T(8,128)S(1)} reduce(f32[256,8,256]{2,1,0:T(8,128)} %bitcast.79, f32[]{:T(128)} %constant.54.clone.1), dimensions={2}, to_apply=%region_5.6 | reduce | flops 522240 | bytes 2105348 | tf_op jit(solution)/shard_map/reduce_sum | solution.py:259
  137.8 0.3 mul.213
  138.2 2.2 %copy.132 = f32[32,8,8,256]{3,1,2,0:T(8,128)} copy(f32[32,8,8,256]{3,2,1,0:T(8,128)S(1)} %bitcast.80) | data formatting | bytes 4194304
  140.4 3.6 %convolution_convert_fusion = bf16[256,512]{1,0:T(8,128)(2,1)} fusion(bf16[2048,512]{1,0:T(8,128)(2,1)} %bitcast.19, f32[256,2048]{1,0:T(8,128)} %bitcast.78, f32[272,2048]{1,0:T(8,128)S(1)} %convert_element_type.89, f32[2048]{0:T(1024)S(1)} %bitcast.94), kind=kOutput, calls=%fused_computation.12 | convolution fusion | flops 538574848 | bytes 6561792 | tf_op jit(solution)/shard_map/dot_general | solution.py:262
  (78 shorter events, 3.1 us)
Async XLA Ops:
  0.6 101.1 %copy-start = (bf16[2,8192]{1,0:T(2,128)(2,1)S(1)}, bf16[2,8192]{1,0:T(2,128)(2,1)}, u32[]{:S(2)}) copy-start(bf16[2,8192]{1,0:T(2,128)(2,1)} %param.18) | copy-start | bytes 98308
  5.6 7.6 %copy-start.6 = (bf16[512]{0:T(512)(128)(2,1)S(1)}, bf16[512]{0:T(512)(128)(2,1)}, u32[]{:S(2)}) copy-start(bf16[512]{0:T(512)(128)(2,1)} %param.16) | copy-start | bytes 3076
  5.6 7.6 %copy-start.3 = (bf16[256,512]{1,0:T(8,128)(2,1)S(1)}, bf16[256,512]{1,0:T(8,128)(2,1)}, u32[]{:S(2)}) copy-start(bf16[256,512]{1,0:T(8,128)(2,1)} %param.15) | copy-start | bytes 786436
  5.6 7.8 %copy-start.7 = (bf16[2,192]{1,0:T(2,128)(2,1)S(1)}, bf16[2,192]{1,0:T(2,128)(2,1)}, u32[]{:S(2)}) copy-start(bf16[2,192]{1,0:T(2,128)(2,1)} %param.22) | copy-start | bytes 2308
  5.6 7.8 %copy-start.4 = (bf16[4,2,192]{2,1,0:T(2,128)(2,1)S(1)}, bf16[4,2,192]{2,1,0:T(2,128)(2,1)}, u32[]{:S(2)}) copy-start(bf16[4,2,192]{2,1,0:T(2,128)(2,1)} %param.21) | copy-start | bytes 9220
  5.7 7.8 %copy-start.5 = (bf16[3,2,192]{2,1,0:T(2,128)(2,1)S(1)}, bf16[3,2,192]{2,1,0:T(2,128)(2,1)}, u32[]{:S(2)}) copy-start(bf16[3,2,192]{2,1,0:T(2,128)(2,1)} %param.23) | copy-start | bytes 6916
  5.7 134.7 %all-to-all-start = ((bf16[128,16,512]{2,0,1:T(8,128)(2,1)}), bf16[128,16,512]{2,0,1:T(8,128)(2,1)}, u32[]{:S(2)}, u32[]{:S(2)}) async-start(bf16[128,16,512]{2,0,1:T(8,128)(2,1)} %copy.116), calls=%async_computation | async-start | bytes 4194304 | tf_op jit(solution)/shard_map/all_to_all | solution.py:193
  100.2 1.5 %copy-start.9 = (f32[2]{0:T(128)S(1)}, f32[2]{0:T(128)}, u32[]{:S(2)}) copy-start(f32[2]{0:T(128)} %param.20) | copy-start | bytes 28
  100.2 1.5 %copy-start.10 = (f32[2]{0:T(128)S(1)}, f32[2]{0:T(128)}, u32[]{:S(2)}) copy-start(f32[2]{0:T(128)} %param.19) | copy-start | bytes 28
  101.2 5.0 %collective-permute-start = (bf16[256,2,128]{0,2,1:T(8,128)(2,1)S(1)}, bf16[256,2,128]{0,2,1:T(8,128)(2,1)S(1)}, u32[]{:S(2)}, u32[]{:S(2)}) collective-permute-start(bf16[256,2,128]{0,2,1:T(8,128)(2,1)S(1)} %slice.93), channel_id=1, source_target_pairs={{0,1},{1,0},{2,3},{3,2},{4,5},{5,4},{6,7},{7,6},{8,9},{9,8},{10,11... | collective-permute-start | bytes 393224 | tf_op jit(solution)/shard_map/ppermute | solution.py:24
  101.7 4.3 %copy-start.11 = (bf16[2,64]{1,0:T(2,128)(2,1)S(1)}, bf16[2,64]{1,0:T(2,128)(2,1)}, u32[]{:S(2)}) copy-start(bf16[2,64]{1,0:T(2,128)(2,1)} %param.26) | copy-start | bytes 772
  105.7 1.7 %copy-start.2 = (f32[2,64,256]{2,1,0:T(8,128)S(1)}, f32[2,64,256]{2,1,0:T(8,128)}, u32[]{:S(2)}) copy-start(f32[2,64,256]{2,1,0:T(8,128)} %param.24) | copy-start | bytes 393220
  107.4 0.7 copy-start.8
  107.7 25.6 %copy-start.1 = (f32[2,64,256]{2,1,0:T(8,128)}, f32[2,64,256]{2,1,0:T(8,128)S(1)}, u32[]{:S(2)}) copy-start(f32[2,64,256]{2,1,0:T(8,128)S(1)} %get-tuple-element.29) | copy-start | bytes 393220

commit v3 on v1

--- a/solution.py
+++ b/solution.py
@@ -1,6 +1,10 @@
+import functools
+
 import jax
 import jax.numpy as jnp
 from jax import lax
+from jax.experimental import pallas as pl
+from jax.experimental.pallas import tpu as pltpu
 from jax.sharding import PartitionSpec as P
 
 P_SIZE = 64
@@ -18,6 +22,134 @@
         if high != low and high < count:
             route += [(low, high), (high, low)]
     return lax.ppermute(block, axis, route)
+
+
+def spread(depth, own_ref, full_ref, local_sem, first_sem, send_sem, recv_sem):
+    me = lax.axis_index("head")
+    row, column, core = me // 4, (me // 2) % 2, me % 2
+    count, width = 4 * depth, own_ref.shape[1]
+    across, beside = me + 2 - 4 * column, me + 1 - 2 * core
+
+    def place(block):
+        return full_ref.at[:, pl.ds(pl.multiple_of(block * width, 128), width)]
+
+    def copy(block, target, sent, source=None):
+        return pltpu.make_async_remote_copy(
+            src_ref=place(block) if source is None else source,
+            dst_ref=place(block),
+            send_sem=sent,
+            recv_sem=recv_sem.at[block],
+            device_id={"head": target},
+            device_id_type=pl.DeviceIdType.MESH,
+        )
+
+    def relay_copy(block, way, source=None):
+        return copy(block, (across, beside)[way], send_sem.at[way, block], source)
+
+    def arrived(block):
+        copy(block, beside, send_sem.at[1, block]).wait_recv()
+
+    def along(start, step):
+        return (start + 4 * step) % count
+
+    barrier = pltpu.get_barrier_semaphore()
+    peers = [along(me, step) for step in range(1, depth)]
+    for target in [across, beside] + peers:
+        pl.semaphore_signal(
+            barrier, inc=1, device_id={"head": target}, device_id_type=pl.DeviceIdType.MESH
+        )
+    pl.semaphore_wait(barrier, depth + 1)
+
+    firsts = [copy(me, peers[k], first_sem.at[k], own_ref) for k in range(depth - 1)]
+    own_relays = [relay_copy(me, way, own_ref) for way in range(2)]
+    for sent in own_relays + firsts:
+        sent.start()
+    keep = pltpu.make_async_copy(own_ref, place(me), local_sem)
+    keep.start()
+
+    relays = []
+
+    def relay(block, ways):
+        arrived(block)
+        for way in ways:
+            passed = relay_copy(block, way)
+            passed.start()
+            relays.append(passed)
+
+    steps = sorted(range(1, depth), key=lambda step: min(step, depth - step))
+    relay(across, (1,))
+    for step in steps:
+        relay(along(me, -step + depth), (0, 1))
+    for step in steps:
+        relay(along(across, -step + depth), (1,))
+    for step in range(depth):
+        arrived(along(beside, step))
+        arrived(along(beside + 2 - 4 * column, step))
+    for sent in firsts + own_relays + relays:
+        sent.wait_send()
+    keep.wait()
+
+
+def gather_columns(block, number):
+    count = lax.axis_size("head")
+    rows, width = block.shape
+    if width % 128 or count % 4 or count > 16:
+        return lax.all_gather(block, "head", axis=1, tiled=True)
+    return pl.pallas_call(
+        functools.partial(spread, count // 4),
+        out_shape=jax.ShapeDtypeStruct((rows, width * count), block.dtype),
+        in_specs=[pl.BlockSpec(memory_space=pltpu.VMEM)],
+        out_specs=pl.BlockSpec(memory_space=pltpu.VMEM),
+        scratch_shapes=[
+            pltpu.SemaphoreType.DMA,
+            pltpu.SemaphoreType.DMA((count // 4,)),
+            pltpu.SemaphoreType.DMA((2, count)),
+            pltpu.SemaphoreType.DMA((count,)),
+        ],
+        compiler_params=pltpu.CompilerParams(
+            collective_id=number, has_side_effects=True, vmem_limit_bytes=24 * 1024 * 1024
+        ),
+        cost_estimate=pl.CostEstimate(
+            flops=0, bytes_accessed=rows * width * count * 16, transcendentals=0
+        ),
+    )(block)
+
+
+def part_share(weights, shard_count, part_count):
+    rows = weights.shape[0] // part_count
+    share = lax.dynamic_slice_in_dim(weights, lax.axis_index("parts") * rows, rows, axis=0)
+    blocks = share.reshape(rows, shard_count, -1).transpose(1, 0, 2)
+    return blocks.reshape(shard_count * rows, -1)
+
+
+def exchange_columns(share, shard_count, part_count):
+    mine = lax.all_to_all(share, "head", split_axis=0, concat_axis=0, tiled=True)
+    mine = mine.reshape(shard_count, -1, mine.shape[1])
+    if part_count != 2:
+        pieces = lax.all_gather(mine, "parts", axis=1)
+    else:
+        other = lax.ppermute(mine, "parts", [(0, 1), (1, 0)])
+        first = lax.axis_index("parts") == 0
+        pieces = jnp.stack(
+            [jnp.where(first, mine, other), jnp.where(first, other, mine)], axis=1
+        )
+    return pieces.reshape(-1, mine.shape[2])
+
+
+def finish(seq_len, gated_ref, weight_ref, out_ref):
+    group_width = gated_ref.shape[1] // G
+    total = jnp.zeros(out_ref.shape, jnp.float32)
+    for group in range(G):
+        span = pl.ds(group * group_width, group_width)
+        gated = gated_ref[pl.ds(0, seq_len), span].astype(jnp.float32)
+        gains = gated_ref[pl.ds(seq_len, 16), span].astype(jnp.float32)[:1]
+        group_sq = jnp.sum(gated * gated, axis=1, keepdims=True)
+        inverse = lax.rsqrt(group_sq / group_width + epsilon)
+        normed = (gated * inverse * gains).astype(jnp.bfloat16)
+        total = total + jnp.dot(
+            normed, weight_ref[span, :], preferred_element_type=jnp.float32
+        )
+    out_ref[...] = total.astype(out_ref.dtype)
 
 
 def halves(values):
@@ -81,19 +213,21 @@
     width_full = w_in.shape[2]
     w_flat = w_in.reshape(-1, width_full)
     contract_last = (((1,), (1,)), ((), ()))
-    w_out_flat = w_out.reshape(-1, w_out.shape[2])
-    w_columns = lax.all_to_all(w_out_flat, "head", split_axis=1, concat_axis=0, tiled=True)
+    shard_count = lax.axis_size("head")
+    part_count = lax.axis_size("parts")
+    w_share = part_share(w_out.reshape(-1, w_out.shape[2]), shard_count, part_count)
     wide_tokens = tokens.astype(jnp.float32)
     gained = (wide_tokens * pre_gain.astype(jnp.float32)).astype(jnp.bfloat16)
     block_width = tokens.shape[1]
-    shard_count = lax.axis_size("head")
     block_sq = jnp.sum(wide_tokens * wide_tokens, axis=1)
     sq_parts = jnp.stack(halves(block_sq)).reshape(-1)
     sq_rows = -(-sq_parts.shape[0] // block_width)
     sq_rows = -(-sq_rows // 16) * 16
     sq_block = jnp.pad(sq_parts, (0, sq_rows * block_width - sq_parts.shape[0]))
     payload = jnp.concatenate([gained, sq_block.reshape(sq_rows, block_width)], axis=0)
-    gathered = lax.all_gather(payload, "head", axis=1, tiled=True)
+    gathered = gather_columns(payload, 1)
+    gathered, w_share = lax.optimization_barrier((gathered, w_share))
+    w_columns = exchange_columns(w_share, shard_count, part_count)
     sq_all = gathered[seq_len:].astype(jnp.float32).reshape(sq_rows, shard_count, block_width)
     sq_all = jnp.sum(sq_all, axis=1).reshape(-1)
     row_sq = sq_all[:seq_len] + sq_all[seq_len : 2 * seq_len]
@@ -126,7 +260,6 @@
             jnp.concatenate([partner_maps, own_maps], axis=1),
             jnp.concatenate([own_maps, partner_maps], axis=1),
         )
-    group_heads = own_maps.shape[1]
     slice_len = own_maps.shape[2] // 2
     b_matrix = own_maps[:, :, :slice_len].reshape(seq_len, -1).astype(jnp.float32)
     c_matrix = own_maps[:, :, slice_len:].reshape(seq_len, -1).astype(jnp.float32)
@@ -145,15 +278,19 @@
         ],
         axis=0,
     )
-    gated_full = lax.all_gather(gated_rows, "head", axis=1, tiled=True).astype(jnp.float32)
-    gains = gated_full[seq_len].reshape(G, -1)
-    gated_groups = gated_full[:seq_len].reshape(seq_len, G, -1)
-    group_sq = jnp.sum(gated_groups * gated_groups, axis=2, keepdims=True)
-    inverse = lax.rsqrt(group_sq / (P_SIZE * group_heads) + epsilon)
-    normed_out = (gated_groups * inverse * gains[None]).astype(jnp.bfloat16)
-    mixer_out = jnp.dot(
-        normed_out.reshape(seq_len, -1), w_columns, preferred_element_type=jnp.float32
-    ).astype(jnp.bfloat16)
+    gated_full = gather_columns(gated_rows, 2)
+    mixer_out = pl.pallas_call(
+        functools.partial(finish, seq_len),
+        out_shape=jax.ShapeDtypeStruct((seq_len, w_columns.shape[1]), jnp.bfloat16),
+        in_specs=[pl.BlockSpec(memory_space=pltpu.VMEM)] * 2,
+        out_specs=pl.BlockSpec(memory_space=pltpu.VMEM),
+        compiler_params=pltpu.CompilerParams(vmem_limit_bytes=40 * 1024 * 1024),
+        cost_estimate=pl.CostEstimate(
+            flops=2 * seq_len * w_columns.size,
+            bytes_accessed=2 * w_columns.size,
+            transcendentals=0,
+        ),
+    )(gated_full, w_columns)
     return (mixer_out, final_state)
 
 

time: 172 us -> 118 us (0.69)
  waiting for transfers between devices: 114 us -> 2.45 us
  Pallas kernels: 0 us -> 53.6 us
  between operations: 14.5 us -> 1.06 us
  local copies, waits for them, and re-layouts: 8.8 us -> 19.9 us
  starting transfers between devices: 7.89 us -> 14.8 us
  matrix products: 16.2 us -> 14.1 us
    all_gather x2 -> x0, waiting for transfers between devices: 113 us -> none  [the longest x1 76.3 us: per_device(): gathered = lax.all_gather(payload, 'head', axis=1, tiled=True)]
    pallas_call x0 -> x3, Pallas kernels: none -> 53.6 us  [the longest x2 52.1 us: gather_columns(): pl.pallas_call(functools.partial(spread, count // 4), out_shape=jax.Shape...]
    all_to_all x1, starting transfers between devices: 7.5 us -> 12.8 us  [exchange_columns(): lax.all_to_all(share, 'head', split_axis=0, concat_axis=0, tiled=True)]
    convert_element_type x2 -> x0, other arithmetic: 2.92 us -> none  [the longest x1 1.61 us: per_device(): lax.all_gather(gated_rows, 'head', axis=1, tiled=True).astype(jnp.float32)]
    dot_general x1 -> x0, matrix products: 2.65 us -> none  [per_device(): jnp.dot(normed_out.reshape(seq_len, -1), w_columns, preferred_element_typ...]
    all_to_all x1 -> x0, local copies, waits for them, and re-layouts: 2.52 us -> none  [per_device(): lax.all_to_all(w_out_flat, 'head', split_axis=1, concat_axis=0, tiled=True)]
    all_to_all x1, waiting for transfers between devices: 0.01 us -> 2.45 us  [exchange_columns(): lax.all_to_all(share, 'head', split_axis=0, concat_axis=0, tiled=True)]
  transfers between devices with their start and end apart: 4 -> 3, of which waited for: 3 -> 1; matrix products, arithmetic and copies ran while one was open for 17% -> 25% of each run, Pallas kernels for 0% -> 15%
where the time goes in v3:
time: 118 us; the launch traced here: 117 us
  Pallas kernels  53.6 us (45%)
  local copies, waits for them, and re-layouts  19.9 us (17%)
  starting transfers between devices  14.8 us (13%)
  matrix products  14.1 us (12%)
  other arithmetic  11 us (9%)
  waiting for transfers between devices  2.45 us (2%)
    pallas_call x2, Pallas kernels, gather_columns(): pl.pallas_call(functools.partial(spread, count // 4), out_shape=jax.Shape...  52.1 us
    all_to_all x1, starting transfers between devices, exchange_columns(): lax.all_to_all(share, 'head', split_axis=0, concat_axis=0, tiled=True)  12.8 us
    dot_general x1, matrix products, per_device(): lax.dot_general(gained_full, w_flat, contract_last, preferred_element_typ...  5.78 us
    dot_general x1, matrix products, per_device(): lax.dot_general(gained_full, w_dt, contract_last, preferred_element_type=...  3.44 us
    unnamed x33, local copies, waits for them, and re-layouts  3.15 us
    all_to_all x1, waiting for transfers between devices, exchange_columns(): lax.all_to_all(share, 'head', split_axis=0, concat_axis=0, tiled=True)  2.45 us
  transfers between devices with their start and end apart: 3, of which 1 were waited for; matrix products, arithmetic and copies ran while one was open for 25% of the time, Pallas kernels for 15%

profile of v3, /device:TPU:0, one launch (start us, length us, event | category | flops | bytes accessed | tf_op | source)
XLA Modules:
  0.0 116.8 jit_solution(1304691740875549534)
XLA Ops:
  1.5 1.1 fusion.19
  3.1 1.6 %copy.40 = bf16[16,64,512]{2,1,0:T(8,128)(2,1)} copy(bf16[16,64,512]{2,0,1:T(8,128)(2,1)S(1)} %bitcast.83) | data formatting | bytes 2097152 | tf_op jit(solution)/shard_map/transpose | solution.py:121
  4.8 34.9 %shard_map.140 = bf16[272,8192]{1,0:T(8,128)(2,1)S(1)} custom-call(bf16[272,512]{1,0:T(8,128)(2,1)S(1)} %pad_maximum_fusion.1.own_ref), custom_call_target="tpu_custom_call" | custom-call | bytes 35651584 | tf_op jit(solution)/shard_map/pallas_call | solution.py:98
  40.1 1.5 %copy-done.1 = bf16[272,8192]{1,0:T(8,128)(2,1)} copy-done((bf16[272,8192]{1,0:T(8,128)(2,1)}, bf16[272,8192]{1,0:T(8,128)(2,1)S(1)}, u32[]{:S(2)}) %copy-start.1) | copy-done | bytes 4456472
  41.7 5.8 %fusion.8 = bf16[256,512]{1,0:T(8,128)(2,1)S(1)} fusion(bf16[512,8192]{1,0:T(8,128)(2,1)} %bitcast.100, bf16[272,8192]{1,0:T(8,128)(2,1)S(1)} %shard_map.140, f32[256]{0:T(256)S(1)} %fusion.56), kind=kOutput, calls=%fused_computation.10 | convolution fusion | flops 2147745792 | bytes 12846080 | tf_op jit(solution)/shard_map/dot_general | solution.py:236
  49.9 12.8 %all-to-all-start = ((bf16[16,64,512]{2,1,0:T(8,128)(2,1)}), bf16[16,64,512]{2,1,0:T(8,128)(2,1)S(1)}, u32[]{:S(2)}, u32[]{:S(2)}) async-start(bf16[16,64,512]{2,1,0:T(8,128)(2,1)} %copy.40), calls=%async_computation | async-start | bytes 2097152 | tf_op jit(solution)/shard_map/all_to_all | solution.py:126
  62.8 3.4 %broadcast_multiply_fusion = (f32[256,2]{0,1:T(2,128)S(1)}, f32[256,2]{0,1:T(2,128)S(1)}) fusion(f32[2]{0:T(128)S(1)} %exponential_negate_fusion, f32[2]{0:T(128)S(1)} %copy-done.12, bf16[2,8192]{1,0:T(2,128)(2,1)S(1)} %copy-done.10, bf16[272,8192]{1,0:T(8,128)(2,1)} %copy-done.1, f32[256]{0:T(256)S(1)} %fusion.56), kind=kOutput, calls=%fused_computation.72 | convolution fusion | flops 8393216 | bytes 4232208 | tf_op jit(solution)/shard_map/dot_general | solution.py:239
  67.0 1.1 reduce_window_sum.11
  68.9 1.6 %fusion.60 = (f32[2,128,2]{2,1,0:T(8,128)}, f32[2,128,2]{2,1,0:T(8,128)}) fusion(f32[2,128,2]{2,1,0:T(8,128)S(1)} %reduce_window_sum.11, f32[2,128,2]{2,1,0:T(8,128)} %bitcast.90, f32[2,2]{1,0:T(2,128)S(1)} %bitcast.94), kind=kLoop, calls=%fused_computation.89 | loop fusion | flops 1024 | bytes 8208 | tf_op jit(solution)/shard_map/exp | solution.py:192
  71.6 1.5 %fusion.59 = (bf16[256,2,64]{0,2,1:T(8,128)(2,1)}, bf16[2,8,2,8,128]{4,3,2,1,0:T(8,128)(2,1)}) fusion(bf16[256,2,192]{0,2,1:T(8,128)(2,1)} %copy-done.4), kind=kLoop, calls=%fused_computation.88 | loop fusion | bytes 196608 | tf_op jit(solution)/shard_map/slice | solution.py:251
  73.1 1.5 %reshape.123 = bf16[2,128,2,64]{1,0,3,2:T(2,128)(2,1)} reshape(bf16[256,2,64]{0,2,1:T(8,128)(2,1)} %get-tuple-element.52) | data formatting | bytes 131072 | tf_op jit(solution)/shard_map/reshape | solution.py:169
  74.6 1.5 %convert_multiply_fusion.3 = f32[2,128,2,64]{1,0,3,2:T(2,128)} fusion(bf16[2,128,2,64]{1,0,3,2:T(2,128)(2,1)} %reshape.123, f32[2,128,2]{1,0,2:T(2,128)S(1)} %copy.51), kind=kLoop, calls=%fused_computation.57 | loop fusion | flops 65536 | bytes 198656 | tf_op jit(solution)/shard_map/cjh,cjhp,cjn->chpn/dot_general | solution.py:181
  77.3 1.6 %copy.55 = f32[2,128,2]{1,2,0:T(2,128)} copy(f32[2,128,2]{2,1,0:T(8,128)} %get-tuple-element.54) | data formatting | bytes 4096 | tf_op jit(solution)/shard_map/exp | solution.py:192
  79.6 1.0 maximum_select_fusion
  82.0 1.2 %fusion.35 = f32[2,2,64,256]{3,2,1,0:T(8,128)S(1)} fusion(bf16[2,128,256,1]{1,0,2,3:T(2,128)(2,1)} %bitcast.86, f32[2,128,2,64]{1,0,3,2:T(2,128)} %convert_multiply_fusion.3), kind=kOutput, calls=%fused_computation.50 | convolution fusion | flops 100663296 | bytes 524288 | tf_op jit(solution)/shard_map/cjh,cjhp,cjn->chpn/dot_general | solution.py:181
  83.2 2.4 %all-to-all-done = bf16[16,64,512]{2,1,0:T(8,128)(2,1)S(1)} async-done(((bf16[16,64,512]{2,1,0:T(8,128)(2,1)}), bf16[16,64,512]{2,1,0:T(8,128)(2,1)S(1)}, u32[]{:S(2)}, u32[]{:S(2)}) %all-to-all-start) | async-done | bytes 1048608 | tf_op jit(solution)/shard_map/all_to_all | solution.py:126
  85.7 1.5 %collective-permute-start.1 = (bf16[16,64,512]{2,1,0:T(8,128)(2,1)S(1)}, bf16[16,64,512]{2,1,0:T(8,128)(2,1)}, u32[]{:S(2)}, u32[]{:S(2)}) collective-permute-start(bf16[16,64,512]{2,1,0:T(8,128)(2,1)S(1)} %all-to-all-done), channel_id=1, source_target_pairs={{0,16},{16,0},{1,17},{17,1},{2,18},{18,2},{3,19},{19,3},{4,20},{20... | collective-permute-start | bytes 3145736 | tf_op jit(solution)/shard_map/ppermute | solution.py:131
  87.2 2.9 %while.12 = (s32[]{:T(128)}, f32[2,64,256]{2,1,0:T(8,128)S(1)}, f32[2,2,64,256]{3,2,1,0:T(8,128)}, f32[2,2]{1,0:T(2,128)}, f32[2,2,64,256]{3,2,1,0:T(8,128)S(1)}, /*index=5*/s32[]{:T(128)}) while((s32[]{:T(128)}, f32[2,64,256]{2,1,0:T(8,128)S(1)}, f32[2,2,64,256]{3,2,1,0:T(8,128)}, f32[2,2]{1,0:T(2,128)}, f32[2,2,64,256]{3,2,1,0:T(8,128)S(1)}, ...), condition=%wide.region_4.5_spmd, body=%wide.region_3.4_spmd.sunk | while | flops 65538 | bytes 655973 | solution.py:190
  91.1 1.1 fusion.39
  92.2 1.3 %convolution_bitcast_fusion = f32[2,128,2,64]{1,3,2,0:T(8,128)S(1)} fusion(f32[2,128,2]{1,2,0:T(2,128)} %bitcast.99, f32[2,128,2]{1,2,0:T(2,128)} %copy.46, f32[2,128,128]{2,1,0:T(8,128)S(1)} %fusion.39, pred[128,128]{1,0:T(8,128)(4,1)S(1)} %iota_compare_fusion, bf16[2,8,2,8,128]{4,3,2,1,0:T(8,128)(2,1)} %get-tuple-element.53), kind=kOutput, calls=%fused_computation.14 | convolution fusion | flops 50659328 | bytes 348160 | tf_op jit(solution)/shard_map/cijh,cjhp->cihp/dot_general | solution.py:179
  93.5 1.2 %fusion.12 = f32[2,2,8,8,128]{4,3,2,1,0:T(8,128)S(1)} fusion(f32[2,128,2,64]{1,3,2,0:T(8,128)S(1)} %convolution_bitcast_fusion, f32[2,2,64,256]{3,2,1,0:T(8,128)} %get-tuple-element.33, bf16[2,128,256,1]{1,0,2,3:T(2,128)(2,1)S(1)} %bitcast.85, f32[2,128,2]{1,2,0:T(2,128)} %copy.55), kind=kOutput, calls=%fused_computation.13 | convolution fusion | flops 100728832 | bytes 657408 | tf_op jit(solution)/shard_map/cin,chpn->cihp/dot_general | solution.py:191
  96.5 17.2 %shard_map.141.gated_ref = bf16[272,2048]{1,0:T(8,128)(2,1)S(1)} custom-call(bf16[272,128]{1,0:T(8,128)(2,1)S(1)} %pad_maximum_fusion.2.own_ref), custom_call_target="tpu_custom_call" | custom-call | bytes 8912896 | tf_op jit(solution)/shard_map/pallas_call | solution.py:98
  113.8 1.4 %select_bitcast_fusion.1 = (bf16[16,1,64,512]{3,2,1,0:T(8,128)(2,1)S(1)}, bf16[16,1,64,512]{3,2,1,0:T(8,128)(2,1)S(1)}) fusion(bf16[16,64,512]{2,1,0:T(8,128)(2,1)S(1)} %all-to-all-done, bf16[16,64,512]{2,1,0:T(8,128)(2,1)} %collective-permute-done.1, pred[]{:T(512)S(6)} %eq.9), kind=kLoop, calls=%fused_computation.18 | loop fusion | flops 1048576 | bytes 4194305 | tf_op jit(solution)/shard_map/stack | solution.py:133
  115.3 1.5 %shard_map.142 = bf16[256,512]{1,0:T(8,128)(2,1)} custom-call(bf16[272,2048]{1,0:T(8,128)(2,1)S(1)} %shard_map.141.gated_ref, bf16[2048,512]{1,0:T(8,128)(2,1)S(1)} %bitcast.81), custom_call_target="tpu_custom_call" | custom-call | flops 536870912 | bytes 2097152 | tf_op jit(solution)/shard_map/pallas_call | solution.py:282
  (77 shorter events, 15.8 us)
Async XLA Ops:
  0.6 2.0 %copy-start = (bf16[2,64,8192]{2,1,0:T(8,128)(2,1)S(1)}, bf16[2,64,8192]{2,1,0:T(8,128)(2,1)}, u32[]{:S(2)}) copy-start(bf16[2,64,8192]{2,1,0:T(8,128)(2,1)} %param.27) | copy-start | bytes 6291460
  39.6 2.0 %copy-start.1 = (bf16[272,8192]{1,0:T(8,128)(2,1)}, bf16[272,8192]{1,0:T(8,128)(2,1)S(1)}, u32[]{:S(2)}) copy-start(bf16[272,8192]{1,0:T(8,128)(2,1)S(1)} %shard_map.140) | copy-start | bytes 13369348
  41.7 6.0 %copy-start.7 = (bf16[3,2,192]{2,1,0:T(2,128)(2,1)S(1)}, bf16[3,2,192]{2,1,0:T(2,128)(2,1)}, u32[]{:S(2)}) copy-start(bf16[3,2,192]{2,1,0:T(2,128)(2,1)} %param.23) | copy-start | bytes 6916
  41.7 6.2 %copy-start.6 = (bf16[4,2,192]{2,1,0:T(2,128)(2,1)S(1)}, bf16[4,2,192]{2,1,0:T(2,128)(2,1)}, u32[]{:S(2)}) copy-start(bf16[4,2,192]{2,1,0:T(2,128)(2,1)} %param.21) | copy-start | bytes 9220
  41.7 6.2 %copy-start.9 = (bf16[2,192]{1,0:T(2,128)(2,1)S(1)}, bf16[2,192]{1,0:T(2,128)(2,1)}, u32[]{:S(2)}) copy-start(bf16[2,192]{1,0:T(2,128)(2,1)} %param.22) | copy-start | bytes 2308
  47.5 15.2 %copy-start.11 = (f32[2]{0:T(128)S(1)}, f32[2]{0:T(128)}, u32[]{:S(2)}) copy-start(f32[2]{0:T(128)} %param.20) | copy-start | bytes 28
  47.5 15.3 %copy-start.10 = (bf16[2,8192]{1,0:T(2,128)(2,1)S(1)}, bf16[2,8192]{1,0:T(2,128)(2,1)}, u32[]{:S(2)}) copy-start(bf16[2,8192]{1,0:T(2,128)(2,1)} %param.18) | copy-start | bytes 98308
  47.5 15.2 %copy-start.12 = (f32[2]{0:T(128)S(1)}, f32[2]{0:T(128)}, u32[]{:S(2)}) copy-start(f32[2]{0:T(128)} %param.19) | copy-start | bytes 28
  47.7 2.3 %copy-start.5 = (bf16[256,512]{0,1:T(8,128)(2,1)}, bf16[256,512]{0,1:T(8,128)(2,1)S(1)}, u32[]{:S(2)}) copy-start(bf16[256,512]{0,1:T(8,128)(2,1)S(1)} %copy.68) | copy-start | bytes 786436
  48.8 0.7 copy-start.4
  49.5 30.1 %collective-permute-start = (bf16[256,2,128]{0,2,1:T(8,128)(2,1)S(1)}, bf16[256,2,128]{0,2,1:T(8,128)(2,1)}, u32[]{:S(2)}, u32[]{:S(2)}) collective-permute-start(bf16[256,2,128]{0,2,1:T(8,128)(2,1)S(1)} %slice.85), channel_id=1, source_target_pairs={{0,1},{1,0},{2,3},{3,2},{4,5},{5,4},{6,7},{7,6},{8,9},{9,8},{10,11... | collective-permute-start | bytes 393224 | tf_op jit(solution)/shard_map/ppermute | solution.py:24
  49.9 29.0 %copy-start.13 = (bf16[2,64]{1,0:T(2,128)(2,1)S(1)}, bf16[2,64]{1,0:T(2,128)(2,1)}, u32[]{:S(2)}) copy-start(bf16[2,64]{1,0:T(2,128)(2,1)} %param.26) | copy-start | bytes 772
  49.9 35.7 %all-to-all-start = ((bf16[16,64,512]{2,1,0:T(8,128)(2,1)}), bf16[16,64,512]{2,1,0:T(8,128)(2,1)S(1)}, u32[]{:S(2)}, u32[]{:S(2)}) async-start(bf16[16,64,512]{2,1,0:T(8,128)(2,1)} %copy.40), calls=%async_computation | async-start | bytes 2097152 | tf_op jit(solution)/shard_map/all_to_all | solution.py:126
  62.8 24.4 %copy-start.3 = (f32[2,64,256]{2,1,0:T(8,128)S(1)}, f32[2,64,256]{2,1,0:T(8,128)}, u32[]{:S(2)}) copy-start(f32[2,64,256]{2,1,0:T(8,128)} %param.24) | copy-start | bytes 393220
  66.2 4.4 %copy-start.8 = (f32[256,2]{0,1:T(2,128)}, f32[256,2]{0,1:T(2,128)S(1)}, u32[]{:S(2)}) copy-start(f32[256,2]{0,1:T(2,128)S(1)} %get-tuple-element.61) | copy-start | bytes 6148
  85.7 28.1 %collective-permute-start.1 = (bf16[16,64,512]{2,1,0:T(8,128)(2,1)S(1)}, bf16[16,64,512]{2,1,0:T(8,128)(2,1)}, u32[]{:S(2)}, u32[]{:S(2)}) collective-permute-start(bf16[16,64,512]{2,1,0:T(8,128)(2,1)S(1)} %all-to-all-done), channel_id=1, source_target_pairs={{0,16},{16,0},{1,17},{17,1},{2,18},{18,2},{3,19},{19,3},{4,20},{20... | collective-permute-start | bytes 3145736 | tf_op jit(solution)/shard_map/ppermute | solution.py:131
  90.1 25.3 %copy-start.2 = (f32[2,64,256]{2,1,0:T(8,128)}, f32[2,64,256]{2,1,0:T(8,128)S(1)}, u32[]{:S(2)}) copy-start(f32[2,64,256]{2,1,0:T(8,128)S(1)} %get-tuple-element.31) | copy-start | bytes 393220

commit v4 on v3

--- a/solution.py
+++ b/solution.py
@@ -90,22 +90,125 @@
     keep.wait()
 
 
-def gather_columns(block, number):
+def spread_hops(depth, cuts, own_ref, full_ref, local_sem, send_sem, recv_sem):
+    me = lax.axis_index("head")
+    row, column, core = me // 4, (me // 2) % 2, me % 2
+    width = own_ref.shape[1]
+    across, beside = me + 2 - 4 * column, me + 1 - 2 * core
+    has_upper, has_lower = row < depth - 1, row > 0
+
+    def place(block, piece):
+        rows = pl.ds(cuts[piece], cuts[piece + 1] - cuts[piece])
+        return full_ref.at[rows, pl.ds(pl.multiple_of(block * width, 128), width)]
+
+    def own_rows(piece):
+        return own_ref.at[pl.ds(cuts[piece], cuts[piece + 1] - cuts[piece])]
+
+    def copy(block, way, target, piece, own=False):
+        return pltpu.make_async_remote_copy(
+            src_ref=own_rows(piece) if own else place(block, piece),
+            dst_ref=place(block, piece),
+            send_sem=send_sem.at[way, piece, block],
+            recv_sem=recv_sem.at[piece, block],
+            device_id={"head": target},
+            device_id_type=pl.DeviceIdType.MESH,
+        )
+
+    def arrived(block, piece):
+        copy(block, 3, beside, piece).wait_recv()
+
+    barrier = pltpu.get_barrier_semaphore()
+
+    def greet(target):
+        pl.semaphore_signal(
+            barrier, inc=1, device_id={"head": target}, device_id_type=pl.DeviceIdType.MESH
+        )
+
+    greet(across)
+    greet(beside)
+    pl.when(has_upper)(lambda: greet(me + 4))
+    pl.when(has_lower)(lambda: greet(me - 4))
+    neighbours = 2 + has_upper.astype(jnp.int32) + has_lower.astype(jnp.int32)
+    pl.semaphore_wait(barrier, neighbours)
+
+    pieces = range(len(cuts) - 1)
+    for piece in pieces:
+        pl.when(has_upper)(lambda: copy(me, 0, me + 4, piece, True).start())
+        pl.when(has_lower)(lambda: copy(me, 1, me - 4, piece, True).start())
+        copy(me, 2, across, piece, True).start()
+        copy(me, 3, beside, piece, True).start()
+    mine = full_ref.at[:, pl.ds(pl.multiple_of(me * width, 128), width)]
+    keep = pltpu.make_async_copy(own_ref, mine, local_sem)
+    keep.start()
+
+    def relay(block, piece):
+        arrived(block, piece)
+        copy(block, 3, beside, piece).start()
+
+    def from_lower(block, piece):
+        arrived(block, piece)
+        pl.when(has_upper)(lambda: copy(block, 0, me + 4, piece).start())
+        copy(block, 2, across, piece).start()
+        copy(block, 3, beside, piece).start()
+
+    def from_upper(block, piece):
+        arrived(block, piece)
+        pl.when(has_lower)(lambda: copy(block, 1, me - 4, piece).start())
+        copy(block, 2, across, piece).start()
+        copy(block, 3, beside, piece).start()
+
+    for apart in range(1, depth):
+        below, above = row - apart >= 0, row + apart < depth
+        for piece in pieces:
+            pl.when(below)(lambda: from_lower(me - 4 * apart, piece))
+            pl.when(above)(lambda: from_upper(me + 4 * apart, piece))
+            if apart == 1:
+                relay(across, piece)
+        for piece in pieces:
+            if apart > 1:
+                pl.when(row - apart + 1 >= 0)(lambda: relay(across - 4 * (apart - 1), piece))
+                pl.when(row + apart - 1 < depth)(lambda: relay(across + 4 * (apart - 1), piece))
+    for piece in pieces:
+        pl.when(row - depth + 1 >= 0)(lambda: relay(across - 4 * (depth - 1), piece))
+        pl.when(row + depth - 1 < depth)(lambda: relay(across + 4 * (depth - 1), piece))
+
+    for piece in pieces:
+        for level in range(depth):
+            for side in range(2):
+                arrived(level * 4 + side * 2 + 1 - core, piece)
+        for level in range(depth):
+            own = level * 4 + column * 2 + core
+            other = level * 4 + (1 - column) * 2 + core
+            pl.when(has_upper & (level <= row))(
+                lambda: copy(own, 0, me + 4, piece, True).wait_send()
+            )
+            pl.when(has_lower & (level >= row))(
+                lambda: copy(own, 1, me - 4, piece, True).wait_send()
+            )
+            copy(own, 2, across, piece, True).wait_send()
+            copy(own, 3, beside, piece, True).wait_send()
+            copy(other, 3, beside, piece, True).wait_send()
+    keep.wait()
+
+
+def gather_columns(block, number, pieces=0):
     count = lax.axis_size("head")
     rows, width = block.shape
     if width % 128 or count % 4 or count > 16:
         return lax.all_gather(block, "head", axis=1, tiled=True)
+    cuts = [-(-rows * piece // (16 * max(pieces, 1))) * 16 for piece in range(pieces + 1)]
+    kernel = functools.partial(spread, count // 4)
+    sems = [(count // 4,), (2, count), (count,)]
+    if pieces:
+        kernel = functools.partial(spread_hops, count // 4, cuts)
+        sems = [(4, pieces, count), (pieces, count)]
     return pl.pallas_call(
-        functools.partial(spread, count // 4),
+        kernel,
         out_shape=jax.ShapeDtypeStruct((rows, width * count), block.dtype),
         in_specs=[pl.BlockSpec(memory_space=pltpu.VMEM)],
         out_specs=pl.BlockSpec(memory_space=pltpu.VMEM),
-        scratch_shapes=[
-            pltpu.SemaphoreType.DMA,
-            pltpu.SemaphoreType.DMA((count // 4,)),
-            pltpu.SemaphoreType.DMA((2, count)),
-            pltpu.SemaphoreType.DMA((count,)),
-        ],
+        scratch_shapes=[pltpu.SemaphoreType.DMA]
+        + [pltpu.SemaphoreType.DMA(sem) for sem in sems],
         compiler_params=pltpu.CompilerParams(
             collective_id=number, has_side_effects=True, vmem_limit_bytes=24 * 1024 * 1024
         ),
@@ -225,7 +328,7 @@
     sq_rows = -(-sq_rows // 16) * 16
     sq_block = jnp.pad(sq_parts, (0, sq_rows * block_width - sq_parts.shape[0]))
     payload = jnp.concatenate([gained, sq_block.reshape(sq_rows, block_width)], axis=0)
-    gathered = gather_columns(payload, 1)
+    gathered = gather_columns(payload, 1, 2)
     gathered, w_share = lax.optimization_barrier((gathered, w_share))
     w_columns = exchange_columns(w_share, shard_count, part_count)
     sq_all = gathered[seq_len:].astype(jnp.float32).reshape(sq_rows, shard_count, block_width)

time: 118 us -> 106 us (0.90)
  starting transfers between devices: 14.8 us -> 6.96 us
  Pallas kernels: 53.6 us -> 49.8 us
    all_to_all x1, starting transfers between devices: 12.8 us -> 4.99 us  [exchange_columns(): lax.all_to_all(share, 'head', split_axis=0, concat_axis=0, tiled=True)]
    pallas_call x2, Pallas kernels: 52.1 us -> 48.3 us  [gather_columns(): pl.pallas_call(kernel, out_shape=jax.ShapeDtypeStruct((rows, width * coun...]
  transfers between devices with their start and end apart: 3 -> 3, of which waited for: 1 -> 1; matrix products, arithmetic and copies ran while one was open for 25% -> 28% of each run, Pallas kernels for 15% -> 16%
where the time goes in v4:
time: 106 us; the launch traced here: 105 us
  Pallas kernels  49.8 us (47%)
  local copies, waits for them, and re-layouts  19.9 us (19%)
  matrix products  14.1 us (13%)
  other arithmetic  11 us (10%)
  starting transfers between devices  6.96 us (7%)
  waiting for transfers between devices  2.45 us (2%)
  between operations  1.06 us (1%)
    pallas_call x2, Pallas kernels, gather_columns(): pl.pallas_call(kernel, out_shape=jax.ShapeDtypeStruct((rows, width * coun...  48.3 us
    dot_general x1, matrix products, per_device(): lax.dot_general(gained_full, w_flat, contract_last, preferred_element_typ...  5.78 us
    all_to_all x1, starting transfers between devices, exchange_columns(): lax.all_to_all(share, 'head', split_axis=0, concat_axis=0, tiled=True)  4.99 us
    dot_general x1, matrix products, per_device(): lax.dot_general(gained_full, w_dt, contract_last, preferred_element_type=...  3.44 us
    unnamed x33, local copies, waits for them, and re-layouts  3.15 us
    all_to_all x1, waiting for transfers between devices, exchange_columns(): lax.all_to_all(share, 'head', split_axis=0, concat_axis=0, tiled=True)  2.45 us
  transfers between devices with their start and end apart: 3, of which 1 were waited for; matrix products, arithmetic and copies ran while one was open for 28% of the time, Pallas kernels for 16%

profile of v4, /device:TPU:0, one launch (start us, length us, event | category | flops | bytes accessed | tf_op | source)
XLA Modules:
  0.0 105.3 jit_solution(9093207343320345177)
XLA Ops:
  1.5 1.1 %fusion.19 = (bf16[256,512]{1,0:T(8,128)(2,1)S(1)}, f32[256]{0:T(256)S(1)}) fusion(bf16[256,512]{1,0:T(8,128)(2,1)} %param.15, f32[512]{0:T(512)S(1)} %convert_element_type.68), kind=kLoop, calls=%fused_computation.21 | loop fusion | flops 655104 | bytes 527360 | tf_op jit(solution)/shard_map/convert_element_type | solution.py:323
  3.1 1.6 %copy.40 = bf16[16,64,512]{2,1,0:T(8,128)(2,1)} copy(bf16[16,64,512]{2,0,1:T(8,128)(2,1)S(1)} %bitcast.83) | data formatting | bytes 2097152 | tf_op jit(solution)/shard_map/transpose | solution.py:224
  4.8 31.3 %shard_map.140 = bf16[272,8192]{1,0:T(8,128)(2,1)S(1)} custom-call(bf16[272,512]{1,0:T(8,128)(2,1)S(1)} %pad_maximum_fusion.1.own_ref), custom_call_target="tpu_custom_call" | custom-call | bytes 35651584 | tf_op jit(solution)/shard_map/pallas_call | solution.py:205
  36.5 1.5 %copy-done.1 = bf16[272,8192]{1,0:T(8,128)(2,1)} copy-done((bf16[272,8192]{1,0:T(8,128)(2,1)}, bf16[272,8192]{1,0:T(8,128)(2,1)S(1)}, u32[]{:S(2)}) %copy-start.1) | copy-done | bytes 4456472
  38.1 5.8 %fusion.8 = bf16[256,512]{1,0:T(8,128)(2,1)S(1)} fusion(bf16[512,8192]{1,0:T(8,128)(2,1)} %bitcast.100, bf16[272,8192]{1,0:T(8,128)(2,1)S(1)} %shard_map.140, f32[256]{0:T(256)S(1)} %fusion.56), kind=kOutput, calls=%fused_computation.10 | convolution fusion | flops 2147745792 | bytes 12846080 | tf_op jit(solution)/shard_map/dot_general | solution.py:339
  46.3 5.0 %all-to-all-start = ((bf16[16,64,512]{2,1,0:T(8,128)(2,1)}), bf16[16,64,512]{2,1,0:T(8,128)(2,1)S(1)}, u32[]{:S(2)}, u32[]{:S(2)}) async-start(bf16[16,64,512]{2,1,0:T(8,128)(2,1)} %copy.40), calls=%async_computation | async-start | bytes 2097152 | tf_op jit(solution)/shard_map/all_to_all | solution.py:229
  51.4 3.4 %broadcast_multiply_fusion = (f32[256,2]{0,1:T(2,128)S(1)}, f32[256,2]{0,1:T(2,128)S(1)}) fusion(f32[2]{0:T(128)S(1)} %exponential_negate_fusion, f32[2]{0:T(128)S(1)} %copy-done.12, bf16[2,8192]{1,0:T(2,128)(2,1)S(1)} %copy-done.10, bf16[272,8192]{1,0:T(8,128)(2,1)} %copy-done.1, f32[256]{0:T(256)S(1)} %fusion.56), kind=kOutput, calls=%fused_computation.72 | convolution fusion | flops 8393216 | bytes 4232208 | tf_op jit(solution)/shard_map/dot_general | solution.py:342
  55.6 1.1 %reduce_window_sum.11 = f32[2,128,2]{2,1,0:T(8,128)S(1)} reduce-window(f32[2,128,2]{2,1,0:T(8,128)} %bitcast.89, f32[]{:T(128)} %constant.56.clone.1), window={size=1x128x1 pad=0_0x127_0x0_0}, to_apply=%region_2.3 | reduce-window | flops 65024 | bytes 4100 | tf_op jit(solution)/shard_map/jit(cumsum)/reduce_window_sum | solution.py:271
  57.5 1.6 %fusion.60 = (f32[2,128,2]{2,1,0:T(8,128)}, f32[2,128,2]{2,1,0:T(8,128)}) fusion(f32[2,128,2]{2,1,0:T(8,128)S(1)} %reduce_window_sum.11, f32[2,128,2]{2,1,0:T(8,128)} %bitcast.90, f32[2,2]{1,0:T(2,128)S(1)} %bitcast.94), kind=kLoop, calls=%fused_computation.89 | loop fusion | flops 1024 | bytes 8208 | tf_op jit(solution)/shard_map/exp | solution.py:295
  60.2 1.5 %fusion.59 = (bf16[256,2,64]{0,2,1:T(8,128)(2,1)}, bf16[2,8,2,8,128]{4,3,2,1,0:T(8,128)(2,1)}) fusion(bf16[256,2,192]{0,2,1:T(8,128)(2,1)} %copy-done.4), kind=kLoop, calls=%fused_computation.88 | loop fusion | bytes 196608 | tf_op jit(solution)/shard_map/slice | solution.py:354
  61.7 1.5 %reshape.123 = bf16[2,128,2,64]{1,0,3,2:T(2,128)(2,1)} reshape(bf16[256,2,64]{0,2,1:T(8,128)(2,1)} %get-tuple-element.52) | data formatting | bytes 131072 | tf_op jit(solution)/shard_map/reshape | solution.py:272
  63.2 1.5 %convert_multiply_fusion.3 = f32[2,128,2,64]{1,0,3,2:T(2,128)} fusion(bf16[2,128,2,64]{1,0,3,2:T(2,128)(2,1)} %reshape.123, f32[2,128,2]{1,0,2:T(2,128)S(1)} %copy.51), kind=kLoop, calls=%fused_computation.57 | loop fusion | flops 65536 | bytes 198656 | tf_op jit(solution)/shard_map/cjh,cjhp,cjn->chpn/dot_general | solution.py:284
  65.9 1.6 %copy.55 = f32[2,128,2]{1,2,0:T(2,128)} copy(f32[2,128,2]{2,1,0:T(8,128)} %get-tuple-element.54) | data formatting | bytes 4096 | tf_op jit(solution)/shard_map/exp | solution.py:295
  68.2 1.0 maximum_select_fusion
  70.6 1.2 %fusion.35 = f32[2,2,64,256]{3,2,1,0:T(8,128)S(1)} fusion(bf16[2,128,256,1]{1,0,2,3:T(2,128)(2,1)} %bitcast.86, f32[2,128,2,64]{1,0,3,2:T(2,128)} %convert_multiply_fusion.3), kind=kOutput, calls=%fused_computation.50 | convolution fusion | flops 100663296 | bytes 524288 | tf_op jit(solution)/shard_map/cjh,cjhp,cjn->chpn/dot_general | solution.py:284
  71.8 2.4 %all-to-all-done = bf16[16,64,512]{2,1,0:T(8,128)(2,1)S(1)} async-done(((bf16[16,64,512]{2,1,0:T(8,128)(2,1)}), bf16[16,64,512]{2,1,0:T(8,128)(2,1)S(1)}, u32[]{:S(2)}, u32[]{:S(2)}) %all-to-all-start) | async-done | bytes 1048608 | tf_op jit(solution)/shard_map/all_to_all | solution.py:229
  74.3 1.5 %collective-permute-start.1 = (bf16[16,64,512]{2,1,0:T(8,128)(2,1)S(1)}, bf16[16,64,512]{2,1,0:T(8,128)(2,1)}, u32[]{:S(2)}, u32[]{:S(2)}) collective-permute-start(bf16[16,64,512]{2,1,0:T(8,128)(2,1)S(1)} %all-to-all-done), channel_id=1, source_target_pairs={{0,16},{16,0},{1,17},{17,1},{2,18},{18,2},{3,19},{19,3},{4,20},{20... | collective-permute-start | bytes 3145736 | tf_op jit(solution)/shard_map/ppermute | solution.py:234
  75.8 2.9 %while.12 = (s32[]{:T(128)}, f32[2,64,256]{2,1,0:T(8,128)S(1)}, f32[2,2,64,256]{3,2,1,0:T(8,128)}, f32[2,2]{1,0:T(2,128)}, f32[2,2,64,256]{3,2,1,0:T(8,128)S(1)}, /*index=5*/s32[]{:T(128)}) while((s32[]{:T(128)}, f32[2,64,256]{2,1,0:T(8,128)S(1)}, f32[2,2,64,256]{3,2,1,0:T(8,128)}, f32[2,2]{1,0:T(2,128)}, f32[2,2,64,256]{3,2,1,0:T(8,128)S(1)}, ...), condition=%wide.region_4.5_spmd, body=%wide.region_3.4_spmd.sunk | while | flops 65538 | bytes 655973 | solution.py:293
  79.7 1.1 %fusion.39 = f32[2,128,128]{2,1,0:T(8,128)S(1)} fusion(bf16[2,128,256]{1,0,2:T(2,128)(2,1)} %reshape.125, bf16[2,128,256]{1,0,2:T(2,128)(2,1)S(1)} %reshape.124), kind=kOutput, calls=%fused_computation.54 | convolution fusion | flops 16777216 | bytes 393216 | tf_op jit(solution)/shard_map/cin,cjn->cij/dot_general | solution.py:280
  80.8 1.3 %convolution_bitcast_fusion = f32[2,128,2,64]{1,3,2,0:T(8,128)S(1)} fusion(f32[2,128,2]{1,2,0:T(2,128)} %bitcast.99, f32[2,128,2]{1,2,0:T(2,128)} %copy.46, f32[2,128,128]{2,1,0:T(8,128)S(1)} %fusion.39, pred[128,128]{1,0:T(8,128)(4,1)S(1)} %iota_compare_fusion, bf16[2,8,2,8,128]{4,3,2,1,0:T(8,128)(2,1)} %get-tuple-element.53), kind=kOutput, calls=%fused_computation.14 | convolution fusion | flops 50659328 | bytes 348160 | tf_op jit(solution)/shard_map/cijh,cjhp->cihp/dot_general | solution.py:282
  82.1 1.2 %fusion.12 = f32[2,2,8,8,128]{4,3,2,1,0:T(8,128)S(1)} fusion(f32[2,128,2,64]{1,3,2,0:T(8,128)S(1)} %convolution_bitcast_fusion, f32[2,2,64,256]{3,2,1,0:T(8,128)} %get-tuple-element.33, bf16[2,128,256,1]{1,0,2,3:T(2,128)(2,1)S(1)} %bitcast.85, f32[2,128,2]{1,2,0:T(2,128)} %copy.55), kind=kOutput, calls=%fused_computation.13 | convolution fusion | flops 100728832 | bytes 657408 | tf_op jit(solution)/shard_map/cin,chpn->cihp/dot_general | solution.py:294
  85.1 17.0 %shard_map.141.gated_ref = bf16[272,2048]{1,0:T(8,128)(2,1)S(1)} custom-call(bf16[272,128]{1,0:T(8,128)(2,1)S(1)} %pad_maximum_fusion.2.own_ref), custom_call_target="tpu_custom_call" | custom-call | bytes 8912896 | tf_op jit(solution)/shard_map/pallas_call | solution.py:205
  102.2 1.4 %select_bitcast_fusion.1 = (bf16[16,1,64,512]{3,2,1,0:T(8,128)(2,1)S(1)}, bf16[16,1,64,512]{3,2,1,0:T(8,128)(2,1)S(1)}) fusion(bf16[16,64,512]{2,1,0:T(8,128)(2,1)S(1)} %all-to-all-done, bf16[16,64,512]{2,1,0:T(8,128)(2,1)} %collective-permute-done.1, pred[]{:T(512)S(6)} %eq.9), kind=kLoop, calls=%fused_computation.18 | loop fusion | flops 1048576 | bytes 4194305 | tf_op jit(solution)/shard_map/stack | solution.py:236
  103.8 1.5 %shard_map.142 = bf16[256,512]{1,0:T(8,128)(2,1)} custom-call(bf16[272,2048]{1,0:T(8,128)(2,1)S(1)} %shard_map.141.gated_ref, bf16[2048,512]{1,0:T(8,128)(2,1)S(1)} %bitcast.81), custom_call_target="tpu_custom_call" | custom-call | flops 536870912 | bytes 2097152 | tf_op jit(solution)/shard_map/pallas_call | solution.py:385
  (77 shorter events, 15.8 us)
Async XLA Ops:
  0.6 2.0 %copy-start = (bf16[2,64,8192]{2,1,0:T(8,128)(2,1)S(1)}, bf16[2,64,8192]{2,1,0:T(8,128)(2,1)}, u32[]{:S(2)}) copy-start(bf16[2,64,8192]{2,1,0:T(8,128)(2,1)} %param.27) | copy-start | bytes 6291460
  36.1 2.0 %copy-start.1 = (bf16[272,8192]{1,0:T(8,128)(2,1)}, bf16[272,8192]{1,0:T(8,128)(2,1)S(1)}, u32[]{:S(2)}) copy-start(bf16[272,8192]{1,0:T(8,128)(2,1)S(1)} %shard_map.140) | copy-start | bytes 13369348
  38.1 6.0 %copy-start.7 = (bf16[3,2,192]{2,1,0:T(2,128)(2,1)S(1)}, bf16[3,2,192]{2,1,0:T(2,128)(2,1)}, u32[]{:S(2)}) copy-start(bf16[3,2,192]{2,1,0:T(2,128)(2,1)} %param.23) | copy-start | bytes 6916
  38.1 6.2 %copy-start.6 = (bf16[4,2,192]{2,1,0:T(2,128)(2,1)S(1)}, bf16[4,2,192]{2,1,0:T(2,128)(2,1)}, u32[]{:S(2)}) copy-start(bf16[4,2,192]{2,1,0:T(2,128)(2,1)} %param.21) | copy-start | bytes 9220
  38.1 6.2 %copy-start.9 = (bf16[2,192]{1,0:T(2,128)(2,1)S(1)}, bf16[2,192]{1,0:T(2,128)(2,1)}, u32[]{:S(2)}) copy-start(bf16[2,192]{1,0:T(2,128)(2,1)} %param.22) | copy-start | bytes 2308
  43.9 7.4 %copy-start.11 = (f32[2]{0:T(128)S(1)}, f32[2]{0:T(128)}, u32[]{:S(2)}) copy-start(f32[2]{0:T(128)} %param.20) | copy-start | bytes 28
  43.9 7.5 %copy-start.10 = (bf16[2,8192]{1,0:T(2,128)(2,1)S(1)}, bf16[2,8192]{1,0:T(2,128)(2,1)}, u32[]{:S(2)}) copy-start(bf16[2,8192]{1,0:T(2,128)(2,1)} %param.18) | copy-start | bytes 98308
  43.9 7.4 %copy-start.12 = (f32[2]{0:T(128)S(1)}, f32[2]{0:T(128)}, u32[]{:S(2)}) copy-start(f32[2]{0:T(128)} %param.19) | copy-start | bytes 28
  44.1 2.3 %copy-start.5 = (bf16[256,512]{0,1:T(8,128)(2,1)}, bf16[256,512]{0,1:T(8,128)(2,1)S(1)}, u32[]{:S(2)}) copy-start(bf16[256,512]{0,1:T(8,128)(2,1)S(1)} %copy.68) | copy-start | bytes 786436
  45.2 0.7 copy-start.4
  45.9 22.3 %collective-permute-start = (bf16[256,2,128]{0,2,1:T(8,128)(2,1)S(1)}, bf16[256,2,128]{0,2,1:T(8,128)(2,1)}, u32[]{:S(2)}, u32[]{:S(2)}) collective-permute-start(bf16[256,2,128]{0,2,1:T(8,128)(2,1)S(1)} %slice.85), channel_id=1, source_target_pairs={{0,1},{1,0},{2,3},{3,2},{4,5},{5,4},{6,7},{7,6},{8,9},{9,8},{10,11... | collective-permute-start | bytes 393224 | tf_op jit(solution)/shard_map/ppermute | solution.py:24
  46.3 21.2 %copy-start.13 = (bf16[2,64]{1,0:T(2,128)(2,1)S(1)}, bf16[2,64]{1,0:T(2,128)(2,1)}, u32[]{:S(2)}) copy-start(bf16[2,64]{1,0:T(2,128)(2,1)} %param.26) | copy-start | bytes 772
  46.3 27.9 %all-to-all-start = ((bf16[16,64,512]{2,1,0:T(8,128)(2,1)}), bf16[16,64,512]{2,1,0:T(8,128)(2,1)S(1)}, u32[]{:S(2)}, u32[]{:S(2)}) async-start(bf16[16,64,512]{2,1,0:T(8,128)(2,1)} %copy.40), calls=%async_computation | async-start | bytes 2097152 | tf_op jit(solution)/shard_map/all_to_all | solution.py:229
  51.4 24.4 %copy-start.3 = (f32[2,64,256]{2,1,0:T(8,128)S(1)}, f32[2,64,256]{2,1,0:T(8,128)}, u32[]{:S(2)}) copy-start(f32[2,64,256]{2,1,0:T(8,128)} %param.24) | copy-start | bytes 393220
  54.8 4.4 %copy-start.8 = (f32[256,2]{0,1:T(2,128)}, f32[256,2]{0,1:T(2,128)S(1)}, u32[]{:S(2)}) copy-start(f32[256,2]{0,1:T(2,128)S(1)} %get-tuple-element.61) | copy-start | bytes 6148
  74.3 27.9 %collective-permute-start.1 = (bf16[16,64,512]{2,1,0:T(8,128)(2,1)S(1)}, bf16[16,64,512]{2,1,0:T(8,128)(2,1)}, u32[]{:S(2)}, u32[]{:S(2)}) collective-permute-start(bf16[16,64,512]{2,1,0:T(8,128)(2,1)S(1)} %all-to-all-done), channel_id=1, source_target_pairs={{0,16},{16,0},{1,17},{17,1},{2,18},{18,2},{3,19},{19,3},{4,20},{20... | collective-permute-start | bytes 3145736 | tf_op jit(solution)/shard_map/ppermute | solution.py:234
  78.7 25.1 %copy-start.2 = (f32[2,64,256]{2,1,0:T(8,128)}, f32[2,64,256]{2,1,0:T(8,128)S(1)}, u32[]{:S(2)}) copy-start(f32[2,64,256]{2,1,0:T(8,128)S(1)} %get-tuple-element.31) | copy-start | bytes 393220
